TPU v7x, 32 devices: a whole 2x2x4 slice. The times are simulated.
32 devices in a mesh: vv: 8 (over z, x), oo: 4 (over y, core).
Axes of the slice: x: 2, y: 2, z: 4, core: 2. Of those that a mesh axis runs over, the one named last changes fastest.
Arguments:
- integrals: bfloat16 [16384, 20480], P('vv', 'oo'), may hold values from -0.0390625 to 0.0390625
- t2: bfloat16 [8, 20480, 1280], P(None, 'oo', 'vv'), may hold values from -6 to 6
- block_owner: int32 [8], replicated, may hold values from 0 to 7, as said below
Outputs:
- residual: float32 [16384, 1280], P('vv', 'oo')
Inputs may be any that keep to these rules, and one draw needn't show every extreme that they name: `block_owner`: each pair irrep 0 to 7 is named by exactly 1 row blocks.
All inputs are finite; a program needn't handle non-finite values.
Results may differ from a plain program's by a relative error of at most 0.0003.
Values may be sent and summed in bfloat16 or wider, within the bound.
No kernel may reach another device: no remote copies, remote signals or barrier semaphores. Data moves between devices by JAX's collectives and lax.ppermute only.
A program may use at most 128 MiB of HBM per device.

v0:
```python
import jax
import jax.numpy as jnp
from jax import lax
from jax.sharding import PartitionSpec as P


def local(integrals, t2, block_owner):
    outgoing = t2[block_owner]
    partial_value = jnp.einsum(
        "rd,sdj->rsj",
        integrals,
        lax.all_to_all(outgoing, "vv", split_axis=0, concat_axis=0, tiled=True),
        preferred_element_type=jnp.float32,
    )
    partial_value = partial_value.reshape(
        partial_value.shape[0], partial_value.shape[1] * partial_value.shape[2]
    )
    return lax.psum_scatter(partial_value, "oo", scatter_dimension=1, tiled=True)


def solution(mesh):
    in_specs = (P("vv", "oo"), P(None, "oo", "vv"), P())
    out_specs = P("vv", "oo")
    return jax.shard_map(local, mesh=mesh, in_specs=in_specs, out_specs=out_specs, check_vma=False)
```

profile of v0, /device:TPU:17, one launch (start us, length us, event | category | flops | bytes accessed | tf_op | source)
XLA Modules:
  0.0 431.7 jit_solution(9661973206639349640)
XLA Ops:
  6.5 0.0 reduce-scatter.2.cloned.1.call-start
  6.5 0.7 compare_select_fusion
  7.2 11.3 %gather_fusion = bf16[8,5120,160]{1,2,0:T(8,128)(2,1)} fusion(bf16[8,5120,160]{1,2,0:T(8,128)(2,1)} %param.4, s32[1024]{0:T(1024)S(1)} %pad_clamp_fusion), kind=kCustom, calls=%fused_computation | custom fusion | bytes 26214432 | tf_op jit(solution)/shard_map/gather | solution.py:8
  18.5 287.6 %all_to_all.5 = bf16[8,5120,160]{1,2,0:T(8,128)(2,1)S(1)} all-to-all(bf16[8,5120,160]{1,2,0:T(8,128)(2,1)} %gather_fusion), channel_id=1, replica_groups=mesh['vv'=8,'oo'=4] {'vv'}, dimensions={0} | all-to-all | bytes 26214400 | tf_op jit(solution)/shard_map/all_to_all | solution.py:12
  306.2 32.1 %fusion = f32[8,160,2048]{2,1,0:T(8,128)} fusion(bf16[8,5120,160]{1,2,0:T(8,128)(2,1)S(1)} %all_to_all.5, bf16[2048,5120]{1,0:T(8,128)(2,1)} %param.3), kind=kOutput, calls=%fused_computation.1 | convolution fusion | flops 26843545600 | bytes 44564480 | tf_op jit(solution)/shard_map/rd,sdj->rsj/dot_general | solution.py:9
  338.2 0.0 reduce-scatter.2.cloned.1.call-update
  338.2 86.7 %reduce-scatter.2.cloned.1.call-done = f32[2048,320]{0,1:T(8,128)} async-done(((f32[2048,1280]{0,1:T(8,128)}), f32[2048,320]{0,1:T(8,128)}) %reduce-scatter.2.cloned.1.call-update) | async-done | bytes 2621456 | tf_op jit(solution)/shard_map/reduce_scatter | solution.py:18
  (1 shorter events, 0.0 us)
Async XLA Ops:
  6.5 418.4 %reduce-scatter.2.cloned.1.call-start = ((), (), s32[]{:S(2)}) async-start(), calls=%async_computation.2 | async-start | bytes 13107200 | tf_op jit(solution)/shard_map/reduce_scatter | solution.py:18
Sparse Core Ops, SparseCore 0:
  338.4 86.5 reduce-scatter.1
where the time goes:
time: 434 us; the launch traced here: 432 us
  blocking collectives  288 us (66%)
  waiting for transfers between devices  86.7 us (20%)
  matrix products  32.1 us (7%)
  between operations  13.4 us (3%)
  local copies, waits for them, and re-layouts  11.3 us (3%)
    all_to_all x1, blocking collectives, local(): lax.all_to_all(outgoing, 'vv', split_axis=0, concat_axis=0, tiled=True)  288 us
    reduce_scatter x1, waiting for transfers between devices, local(): lax.psum_scatter(partial_value, 'oo', scatter_dimension=1, tiled=True)  86.7 us
    dot_general x1, matrix products, local(): jnp.einsum('rd,sdj->rsj', integrals, lax.all_to_all(outgoing, 'vv', split...  32.1 us
    gather x1, local copies, waits for them, and re-layouts, local(): outgoing = t2[block_owner]  11.3 us
  transfers between devices with their start and end apart: 1, of which 1 were waited for; matrix products, arithmetic and copies ran while one was open for 0% of the time, Pallas kernels for 0%

commit v1 on v0

v1 whole, which is shorter than its diff:
```python
import math

import jax
import jax.numpy as jnp
from jax import lax
from jax.experimental import pallas as pl
from jax.experimental.pallas import tpu as pltpu
from jax.sharding import PartitionSpec as P

BLOCK = 512
LINK_SHARE = 64
CUT = 80


def cut_kernel(owner, me, *refs):
    n = len(refs) // 2
    for block, out in zip(refs[:n], refs[n:]):
        out[...] = block[0]


def cut(parts, owner, me, blocks):
    depth = blocks.shape[2]
    _, start, width = parts[0]
    step = math.gcd(math.gcd(start, width), CUT)
    return pl.pallas_call(
        cut_kernel,
        grid_spec=pltpu.PrefetchScalarGridSpec(
            num_scalar_prefetch=2,
            grid=(width // step,),
            in_specs=[
                pl.BlockSpec((1, step, depth), lambda i, owner, me, mask=mask: (owner[me[0] ^ mask], start // step + i, 0))
                for mask, _, _ in parts
            ],
            out_specs=[pl.BlockSpec((step, depth), lambda i, owner, me: (i, 0))] * len(parts),
        ),
        out_shape=[jax.ShapeDtypeStruct((width, depth), blocks.dtype)] * len(parts),
        cost_estimate=pl.CostEstimate(flops=0, bytes_accessed=4 * depth * width * len(parts), transcendentals=0),
        compiler_params=pltpu.CompilerParams(vmem_limit_bytes=56 * 2**20),
    )(owner, me, *[blocks] * len(parts))


def product_kernel(*refs):
    *pieces, rows, out, held = refs

    @pl.when(pl.program_id(0) == 0)
    def _():
        at = 0
        for piece in pieces:
            held[at : at + piece.shape[0], :] = piece[...]
            at += piece.shape[0]

    out[...] = lax.dot_general(held[...], rows[...], (((1,), (1,)), ((), ())), preferred_element_type=jnp.float32)


def product(pieces, integrals):
    depth, rows = pieces[0].shape[1], integrals.shape[0]
    n = sum(piece.shape[0] for piece in pieces)
    block = min(BLOCK, rows)
    return pl.pallas_call(
        product_kernel,
        grid=(rows // block,),
        in_specs=[pl.BlockSpec(piece.shape, lambda i: (0, 0)) for piece in pieces]
        + [pl.BlockSpec((block, depth), lambda i: (i, 0))],
        out_specs=pl.BlockSpec((n, block), lambda i: (0, i)),
        out_shape=jax.ShapeDtypeStruct((n, rows), jnp.float32),
        scratch_shapes=[pltpu.VMEM((n, depth), pieces[0].dtype)],
        cost_estimate=pl.CostEstimate(
            flops=2 * n * depth * rows // LINK_SHARE,
            bytes_accessed=(2 * (n + rows) * depth + 4 * n * rows) // LINK_SHARE,
            transcendentals=0,
        ),
        compiler_params=pltpu.CompilerParams(vmem_limit_bytes=48 * 2**20),
    )(*pieces, integrals)


def after(xs, *others):
    return list(lax.optimization_barrier((*xs, *others))[: len(xs)])


def local(vv, oo, integrals, t2, block_owner):
    v, o = lax.axis_index("vv"), lax.axis_index("oo")
    blocks = jnp.swapaxes(t2, 1, 2)
    columns, rows = blocks.shape[1], integrals.shape[0]
    ratio = vv // oo
    offset = (v // ratio) ^ o
    me = v.reshape(1)
    half, quarter = vv // 2, vv // 4

    top = oo // 2
    bits = [1 << k for k in range(top.bit_length() - 1)]
    whole = {mask: (mask, 0, columns) for mask in range(vv)}
    first = [whole[mask] for mask in [*range(half, half + quarter), *range(1, half)]]
    second = [whole[mask] for mask in range(half + quarter, vv)]
    ready = {}
    for some in (first[:quarter], [*first[quarter:], whole[0], *second]):
        ready.update(zip(some, cut(some, block_owner, me, blocks)))
    got = {whole[0]: ready[whole[0]]}

    def fetch(parts, *before):
        sent = [ready[part] for part in parts]
        for part, x in zip(parts, after(sent, *before) if before else sent):
            got[part] = lax.ppermute(x, "vv", [(i, i ^ part[0]) for i in range(vv)])

    made = []

    def multiply(parts, *before):
        made.append(product(after([got[part] for part in parts], *made[-1:], *before), integrals))
        return made[-1]

    def hop(x, j, bit):
        pairs = [
            (a * oo + b, a * oo + (b ^ bit))
            for a in range(vv)
            for b in range(oo)
            if ((a // ratio) ^ b ^ j) % (2 * bit) == bit
        ]
        return lax.ppermute(x, ("vv", "oo"), pairs)

    def inner(each):
        for part in each:
            for bit in bits:
                each[part] = each[part] + hop(each[part], part[0] // ratio, bit)
        return each

    def outer(each):
        return {part: x + hop(x, part[0] // ratio, top) for part, x in each.items()}

    def fold(x):
        for bit in bits:
            mine = (offset // bit) % 2 == 1
            n = x[0].shape[0]
            sent = jnp.concatenate([jnp.where(mine, one, two) for one, two in zip(x[::2], x[1::2])])
            came = lax.ppermute(sent, "oo", [(i, i ^ bit) for i in range(oo)])
            x = [jnp.where(mine, two, one) + came[i * n : (i + 1) * n] for i, (one, two) in enumerate(zip(x[::2], x[1::2]))]
        return x[0]

    def place(out, x, part, mine):
        row = ((v ^ part[0]) % ratio) * columns + part[1]
        return lax.dynamic_update_slice(out, jnp.where(mine, x, lax.dynamic_slice(out, (row, 0), x.shape)), (row, 0))

    fetch(first)
    fetch(second[:-1], *[got[part] for part in first[:quarter]])
    middle = [got[part] for part in second[:-1]]
    fetch(second[-1:], *middle)
    near = []
    for j in range(top):
        arrived = [got[part] for part in first[: quarter * (j + 1) // top]]
        near.append(multiply([whole[mask] for mask in range(j * ratio, (j + 1) * ratio)], *arrived))
    early = {}
    for j in range(top, top + top // 2):
        early[j * ratio, 0, ratio * columns] = multiply([whole[mask] for mask in range(j * ratio, (j + 1) * ratio)])
    near = fold(near)
    early = inner(dict(zip(early, after(list(early.values()), *middle))))
    pairs = [(a * oo + b, a * oo + (b ^ top)) for a in range(vv) for b in range(oo) if ((a // ratio) ^ b) & top]
    near = near + lax.ppermute(near, ("vv", "oo"), pairs)
    early = outer(early)
    late, before = {}, []
    for part in second:
        if part == second[-1]:
            before += [near, *early.values()]
        sums = inner({part: multiply([part], *before)})
        before = list(sums.values())
        late.update(outer(sums))

    out = jnp.zeros((ratio * columns, rows), jnp.float32)
    for low in range(ratio):
        rows_of = slice(low * columns, (low + 1) * columns)
        out = place(out, near[rows_of], whole[low], offset < top)
        for part, x in early.items():
            out = place(out, x[rows_of], whole[part[0] + low], offset == part[0] // ratio)
    for part, x in late.items():
        out = place(out, x, part, offset == part[0] // ratio)
    return out.T


def solution(mesh):
    vv, oo = mesh.shape["vv"], mesh.shape["oo"]
    in_specs = (P("vv", "oo"), P(None, "oo", "vv"), P())
    return jax.shard_map(
        lambda *a: local(vv, oo, *a), mesh=mesh, in_specs=in_specs, out_specs=P("vv", "oo"), check_vma=False
    )
```

time: 434 us -> 353 us (0.81)
  blocking collectives: 288 us -> 0 us
  waiting for transfers between devices: 86.7 us -> 235 us
  Pallas kernels: 0 us -> 68 us
  matrix products: 32.1 us -> 0 us
  starting transfers between devices: 0.01 us -> 27.7 us
  other arithmetic: 0.67 us -> 15.7 us
  between operations: 13.4 us -> 0.37 us
  local copies, waits for them, and re-layouts: 11.3 us -> 4.97 us
    all_to_all x1 -> x0, blocking collectives: 288 us -> none  [local(): lax.all_to_all(outgoing, 'vv', split_axis=0, concat_axis=0, tiled=True)]
    ppermute x0 -> x15, waiting for transfers between devices: none -> 235 us  [the longest x7 169 us: fetch(): got[part] = lax.ppermute(x, 'vv', [(i, i ^ part[0]) for i in range(vv)])]
    reduce_scatter x1 -> x0, waiting for transfers between devices: 86.7 us -> none  [local(): lax.psum_scatter(partial_value, 'oo', scatter_dimension=1, tiled=True)]
    pallas_call x0 -> x7, Pallas kernels: none -> 68 us  [the longest x5 56.7 us: product(): pl.pallas_call(product_kernel, grid=(rows // block,), in_specs=[pl.BlockS...]
    dot_general x1 -> x0, matrix products: 32.1 us -> none  [local(): jnp.einsum('rd,sdj->rsj', integrals, lax.all_to_all(outgoing, 'vv', split...]
    ppermute x0 -> x15, starting transfers between devices: none -> 27.7 us  [the longest x6 10.9 us: hop(): return lax.ppermute(x, ('vv', 'oo'), pairs)]
    add x0 -> x6, other arithmetic: none -> 13.7 us  [the longest x1 4.14 us: fold(): jnp.where(mine, two, one) + came[i * n:(i + 1) * n]]
    gather x1 -> x0, local copies, waits for them, and re-layouts: 11.3 us -> none  [local(): outgoing = t2[block_owner]]
  transfers between devices with their start and end apart: 1 -> 15, of which waited for: 1 -> 10; matrix products, arithmetic and copies ran while one was open for 0% -> 4% of each run, Pallas kernels for 0% -> 15%
where the time goes in v1:
time: 353 us; the launch traced here: 352 us
  waiting for transfers between devices  235 us (67%)
  Pallas kernels  68 us (19%)
  starting transfers between devices  27.7 us (8%)
  other arithmetic  15.7 us (4%)
  local copies, waits for them, and re-layouts  4.97 us (1%)
    ppermute x7, waiting for transfers between devices, fetch(): got[part] = lax.ppermute(x, 'vv', [(i, i ^ part[0]) for i in range(vv)])  169 us
    pallas_call x5, Pallas kernels, product(): pl.pallas_call(product_kernel, grid=(rows // block,), in_specs=[pl.BlockS...  56.7 us
    ppermute x1, waiting for transfers between devices, local(): near = near + lax.ppermute(near, ('vv', 'oo'), pairs)  36 us
    ppermute x6, waiting for transfers between devices, hop(): return lax.ppermute(x, ('vv', 'oo'), pairs)  29.7 us
    pallas_call x2, Pallas kernels, cut(): pl.pallas_call(cut_kernel, grid_spec=pltpu.PrefetchScalarGridSpec(num_sca...  11.3 us
    ppermute x6, starting transfers between devices, hop(): return lax.ppermute(x, ('vv', 'oo'), pairs)  10.9 us
    ppermute x7, starting transfers between devices, fetch(): got[part] = lax.ppermute(x, 'vv', [(i, i ^ part[0]) for i in range(vv)])  10.8 us
  transfers between devices with their start and end apart: 15, of which 10 were waited for; matrix products, arithmetic and copies ran while one was open for 4% of the time, Pallas kernels for 15%

profile of v1, /device:TPU:17, one launch (start us, length us, event | category | flops | bytes accessed | tf_op | source)
XLA Modules:
  0.0 351.8 jit_solution(1490647553150274937)
XLA Ops:
  0.0 3.9 %shard_map.38 = (bf16[160,5120]{1,0:T(8,128)(2,1)}, bf16[160,5120]{1,0:T(8,128)(2,1)}) custom-call(s32[8]{0:T(128)} %owner.3, s32[1]{0:T(128)} %bitcast.me, bf16[8,160,5120]{2,1,0:T(8,128)(2,1)} %bitcast.3, bf16[8,160,5120]{2,1,0:T(8,128)(2,1)} %bitcast.4), custom_call_target="tpu_custom_call" | custom-call | bytes 6553600 | tf_op jit(solution)/shard_map/pallas_call | solution.py:25
  3.9 3.3 collective-permute-start.4
  7.2 7.4 %shard_map.37 = (bf16[160,5120]{1,0:T(8,128)(2,1)}, bf16[160,5120]{1,0:T(8,128)(2,1)}, bf16[160,5120]{1,0:T(8,128)(2,1)}, bf16[160,5120]{1,0:T(8,128)(2,1)}, bf1...) custom-call(s32[8]{0:T(128)} %owner.3, s32[1]{0:T(128)} %bitcast.me, bf16[8,160,5120]{2,1,0:T(8,128)(2,1)} %bitcast.5, ...), custom_call_target="tpu_custom_call" | custom-call | bytes 19660800 | tf_op jit(solution)/shard_map/pallas_call | solution.py:25
  14.9 1.3 collective-permute-start
  17.3 92.0 %collective-permute-done.3.refs_0_ = bf16[160,5120]{1,0:T(8,128)(2,1)S(1)} collective-permute-done((bf16[160,5120]{1,0:T(8,128)(2,1)}, bf16[160,5120]{1,0:T(8,128)(2,1)S(1)}, u32[]{:S(2)}, u32[]{:S(2)}) %collective-permute-start.3) | collective-permute-done | bytes 1638432 | tf_op jit(solution)/shard_map/ppermute | solution.py:102
  109.3 35.1 %collective-permute-done.4.refs_1_ = bf16[160,5120]{1,0:T(8,128)(2,1)S(1)} collective-permute-done((bf16[160,5120]{1,0:T(8,128)(2,1)}, bf16[160,5120]{1,0:T(8,128)(2,1)S(1)}, u32[]{:S(2)}, u32[]{:S(2)}) %collective-permute-start.4) | collective-permute-done | bytes 1638432 | tf_op jit(solution)/shard_map/ppermute | solution.py:102
  145.6 3.1 collective-permute-start.7
  148.7 1.4 copy-done.2
  150.2 11.6 %shard_map.39 = f32[320,2048]{1,0:T(8,128)S(1)} custom-call(bf16[160,5120]{1,0:T(8,128)(2,1)S(1)} %copy-done.2, bf16[160,5120]{1,0:T(8,128)(2,1)} %collective-permute-done.2.refs_1_, bf16[2048,5120]{1,0:T(8,128)(2,1)} %refs_1_.3), custom_call_target="tpu_custom_call" | custom-call | flops 104857600 | bytes 419840 | tf_op jit(solution)/shard_map/pallas_call | solution.py:59
  161.8 28.6 %collective-permute-done.1.refs_1_ = bf16[160,5120]{1,0:T(8,128)(2,1)} collective-permute-done((bf16[160,5120]{1,0:T(8,128)(2,1)}, bf16[160,5120]{1,0:T(8,128)(2,1)}, u32[]{:S(2)}, u32[]{:S(2)}) %collective-permute-start.1) | collective-permute-done | bytes 1638432 | tf_op jit(solution)/shard_map/ppermute | solution.py:102
  190.4 12.1 %shard_map.40 = f32[320,2048]{1,0:T(8,128)S(1)} custom-call(bf16[160,5120]{1,0:T(8,128)(2,1)} %collective-permute-done.refs_0_, bf16[160,5120]{1,0:T(8,128)(2,1)} %collective-permute-done.1.refs_1_, bf16[2048,5120]{1,0:T(8,128)(2,1)} %refs_1_.3), custom_call_target="tpu_custom_call" | custom-call | flops 104857600 | bytes 419840 | tf_op jit(solution)/shard_map/pallas_call | solution.py:59
  203.0 2.5 collective-permute-start.5
  205.5 11.1 %shard_map.41 = f32[320,2048]{1,0:T(8,128)S(1)} custom-call(bf16[160,5120]{1,0:T(8,128)(2,1)S(1)} %collective-permute-done.3.refs_0_, bf16[160,5120]{1,0:T(8,128)(2,1)S(1)} %copy-done.1, bf16[2048,5120]{1,0:T(8,128)(2,1)} %refs_1_.3), custom_call_target="tpu_custom_call" | custom-call | flops 104857600 | bytes 419840 | tf_op jit(solution)/shard_map/pallas_call | solution.py:59
  216.6 3.1 collective-permute-done.7.refs_0_
  219.8 3.1 collective-permute-start.8
  222.9 4.1 %select_add_fusion = f32[320,2048]{1,0:T(8,128)} fusion(f32[320,2048]{1,0:T(8,128)} %collective-permute-done.5, f32[320,2048]{1,0:T(8,128)S(1)} %shard_map.40, f32[320,2048]{1,0:T(8,128)S(1)} %shard_map.39, pred[]{:T(512)S(6)} %eq.19), kind=kLoop, calls=%fused_computation | loop fusion | flops 1310720 | bytes 10485761 | tf_op jit(solution)/shard_map/add | solution.py:134
  227.0 3.4 collective-permute-start.6
  231.0 2.2 collective-permute-start.9
  233.2 1.7 collective-permute-start.12
  235.0 10.9 %shard_map.42 = f32[160,2048]{1,0:T(8,128)S(1)} custom-call(bf16[160,5120]{1,0:T(8,128)(2,1)S(1)} %collective-permute-done.7.refs_0_, bf16[2048,5120]{1,0:T(8,128)(2,1)} %refs_1_.3), custom_call_target="tpu_custom_call" | custom-call | flops 52428800 | bytes 373760 | tf_op jit(solution)/shard_map/pallas_call | solution.py:59
  245.9 1.5 collective-permute-start.10
  247.4 3.4 collective-permute-done.10
  251.0 36.0 %collective-permute-done.6 = f32[320,2048]{1,0:T(8,128)S(1)} collective-permute-done((f32[320,2048]{1,0:T(8,128)}, f32[320,2048]{1,0:T(8,128)S(1)}, u32[]{:S(2)}, u32[]{:S(2)}) %collective-permute-start.6) | collective-permute-done | bytes 2621472 | tf_op jit(solution)/shard_map/ppermute | solution.py:155
  287.0 3.7 %add.73 = f32[320,2048]{1,0:T(8,128)} add(f32[320,2048]{1,0:T(8,128)} %select_add_fusion, f32[320,2048]{1,0:T(8,128)S(1)} %collective-permute-done.6) | non-fusion elementwise | flops 655360 | bytes 7864320 | tf_op jit(solution)/shard_map/add | solution.py:155
  290.7 3.7 %add.77 = f32[320,2048]{1,0:T(8,128)} add(f32[320,2048]{1,0:T(8,128)S(1)} %add.76, f32[320,2048]{1,0:T(8,128)} %collective-permute-done.9) | non-fusion elementwise | flops 655360 | bytes 7864320 | tf_op jit(solution)/shard_map/add | solution.py:126
  294.4 10.5 %collective-permute-done.12.refs_0_ = bf16[160,5120]{1,0:T(8,128)(2,1)S(1)} collective-permute-done((bf16[160,5120]{1,0:T(8,128)(2,1)S(1)}, bf16[160,5120]{1,0:T(8,128)(2,1)S(1)}, u32[]{:S(2)}, u32[]{:S(2)}) %collective-permute-start.12) | collective-permute-done | bytes 1638432 | tf_op jit(solution)/shard_map/ppermute | solution.py:102
  304.9 10.9 %shard_map.43 = f32[160,2048]{1,0:T(8,128)S(1)} custom-call(bf16[160,5120]{1,0:T(8,128)(2,1)S(1)} %collective-permute-done.12.refs_0_, bf16[2048,5120]{1,0:T(8,128)(2,1)} %refs_1_.3), custom_call_target="tpu_custom_call" | custom-call | flops 52428800 | bytes 373760 | tf_op jit(solution)/shard_map/pallas_call | solution.py:59
  317.3 1.6 collective-permute-start.11
  320.9 1.5 add.88
  324.2 11.7 %collective-permute-done.11 = f32[160,2048]{1,0:T(8,128)S(1)} collective-permute-done((f32[160,2048]{1,0:T(8,128)S(1)}, f32[160,2048]{1,0:T(8,128)S(1)}, u32[]{:S(2)}, u32[]{:S(2)}) %collective-permute-start.11) | collective-permute-done | bytes 1310752 | tf_op jit(solution)/shard_map/ppermute | solution.py:117
  336.3 13.7 %collective-permute-done.14 = f32[160,2048]{1,0:T(8,128)S(1)} collective-permute-done((f32[160,2048]{1,0:T(8,128)S(1)}, f32[160,2048]{1,0:T(8,128)S(1)}, u32[]{:S(2)}, u32[]{:S(2)}) %collective-permute-start.14) | collective-permute-done | bytes 1310752 | tf_op jit(solution)/shard_map/ppermute | solution.py:117
  350.3 1.5 copy-done.3
  (33 shorter events, 9.5 us)
Async XLA Ops:
  3.9 105.4 %collective-permute-start.3 = (bf16[160,5120]{1,0:T(8,128)(2,1)}, bf16[160,5120]{1,0:T(8,128)(2,1)S(1)}, u32[]{:S(2)}, u32[]{:S(2)}) collective-permute-start(bf16[160,5120]{1,0:T(8,128)(2,1)} %get-tuple-element.28), channel_id=1, source_target_pairs={{0,16},{4,20},{8,24},{12,28},{16,0},{20,4},{24,8},{28,12},{1,17},{... | collective-permute-start | bytes 4915208 | tf_op jit(solution)/shard_map/ppermute | solution.py:102
  3.9 140.5 %collective-permute-start.4 = (bf16[160,5120]{1,0:T(8,128)(2,1)}, bf16[160,5120]{1,0:T(8,128)(2,1)S(1)}, u32[]{:S(2)}, u32[]{:S(2)}) collective-permute-start(bf16[160,5120]{1,0:T(8,128)(2,1)} %get-tuple-element.31), channel_id=1, source_target_pairs={{0,20},{4,16},{8,28},{12,24},{16,4},{20,0},{24,12},{28,8},{1,21},{... | collective-permute-start | bytes 4915208 | tf_op jit(solution)/shard_map/ppermute | solution.py:102
  14.6 134.1 %collective-permute-start.2 = (bf16[160,5120]{1,0:T(8,128)(2,1)}, bf16[160,5120]{1,0:T(8,128)(2,1)}, u32[]{:S(2)}, u32[]{:S(2)}) collective-permute-start(bf16[160,5120]{1,0:T(8,128)(2,1)} %get-tuple-element.27), channel_id=1, source_target_pairs={{0,4},{4,0},{8,12},{12,8},{16,20},{20,16},{24,28},{28,24},{1,5},{5... | collective-permute-start | bytes 4915208 | tf_op jit(solution)/shard_map/ppermute | solution.py:102
  14.9 146.9 %collective-permute-start = (bf16[160,5120]{1,0:T(8,128)(2,1)}, bf16[160,5120]{1,0:T(8,128)(2,1)}, u32[]{:S(2)}, u32[]{:S(2)}) collective-permute-start(bf16[160,5120]{1,0:T(8,128)(2,1)} %get-tuple-element.24), channel_id=1, source_target_pairs={{0,8},{4,12},{8,0},{12,4},{16,24},{20,28},{24,16},{28,20},{1,9},{5... | collective-permute-start | bytes 4915208 | tf_op jit(solution)/shard_map/ppermute | solution.py:102
  16.2 174.2 %collective-permute-start.1 = (bf16[160,5120]{1,0:T(8,128)(2,1)}, bf16[160,5120]{1,0:T(8,128)(2,1)}, u32[]{:S(2)}, u32[]{:S(2)}) collective-permute-start(bf16[160,5120]{1,0:T(8,128)(2,1)} %get-tuple-element.25), channel_id=1, source_target_pairs={{0,12},{4,8},{8,4},{12,0},{16,28},{20,24},{24,20},{28,16},{1,13},{... | collective-permute-start | bytes 4915208 | tf_op jit(solution)/shard_map/ppermute | solution.py:102
  144.4 1.2 copy-start
  145.6 74.2 %collective-permute-start.7 = (bf16[160,5120]{1,0:T(8,128)(2,1)}, bf16[160,5120]{1,0:T(8,128)(2,1)S(1)}, u32[]{:S(2)}, u32[]{:S(2)}) collective-permute-start(bf16[160,5120]{1,0:T(8,128)(2,1)} %get-tuple-element.37), channel_id=1, source_target_pairs={{0,24},{4,28},{8,16},{12,20},{16,8},{20,12},{24,0},{28,4},{1,25},{... | collective-permute-start | bytes 4915208 | tf_op jit(solution)/shard_map/ppermute | solution.py:102
  148.7 1.4 copy-start.2
  202.5 3.0 copy-start.1
  203.0 19.8 %collective-permute-start.5 = (f32[320,2048]{1,0:T(8,128)S(1)}, f32[320,2048]{1,0:T(8,128)}, u32[]{:S(2)}, u32[]{:S(2)}) collective-permute-start(f32[320,2048]{1,0:T(8,128)S(1)} %broadcast_select_fusion), channel_id=1, source_target_pairs={{0,1},{1,0},{2,3},{3,2},{4,5},{5,4},{6,7},{7,6},{8,9},{9,8},{10,11... | collective-permute-start | bytes 7864328 | tf_op jit(solution)/shard_map/ppermute | solution.py:133
  219.8 10.7 %collective-permute-start.8 = (f32[320,2048]{1,0:T(8,128)S(1)}, f32[320,2048]{1,0:T(8,128)S(1)}, u32[]{:S(2)}, u32[]{:S(2)}) collective-permute-start(f32[320,2048]{1,0:T(8,128)S(1)} %shard_map.41), channel_id=1, source_target_pairs={{1,0},{3,2},{5,4},{7,6},{8,9},{10,11},{12,13},{14,15},{17,16},{19,... | collective-permute-start | bytes 7864328 | tf_op jit(solution)/shard_map/ppermute | solution.py:117
  227.0 6.2 %copy-start.6 = (bf16[160,5120]{1,0:T(8,128)(2,1)S(1)}, bf16[160,5120]{1,0:T(8,128)(2,1)}, u32[]{:S(2)}) copy-start(bf16[160,5120]{1,0:T(8,128)(2,1)} %get-tuple-element.41) | copy-start | bytes 4915204
  227.0 59.9 %collective-permute-start.6 = (f32[320,2048]{1,0:T(8,128)}, f32[320,2048]{1,0:T(8,128)S(1)}, u32[]{:S(2)}, u32[]{:S(2)}) collective-permute-start(f32[320,2048]{1,0:T(8,128)} %select_add_fusion), channel_id=1, source_target_pairs={{2,0},{3,1},{6,4},{7,5},{10,8},{11,9},{14,12},{15,13},{16,18},{17,... | collective-permute-start | bytes 7864328 | tf_op jit(solution)/shard_map/ppermute | solution.py:155
  231.0 59.7 %collective-permute-start.9 = (f32[320,2048]{1,0:T(8,128)S(1)}, f32[320,2048]{1,0:T(8,128)}, u32[]{:S(2)}, u32[]{:S(2)}) collective-permute-start(f32[320,2048]{1,0:T(8,128)S(1)} %add.76), channel_id=1, source_target_pairs={{0,2},{4,6},{9,11},{13,15},{18,16},{22,20},{27,25},{31,29}} | collective-permute-start | bytes 7864328 | tf_op jit(solution)/shard_map/ppermute | solution.py:117
  233.2 71.7 %collective-permute-start.12 = (bf16[160,5120]{1,0:T(8,128)(2,1)S(1)}, bf16[160,5120]{1,0:T(8,128)(2,1)S(1)}, u32[]{:S(2)}, u32[]{:S(2)}) collective-permute-start(bf16[160,5120]{1,0:T(8,128)(2,1)S(1)} %copy-done.6), channel_id=1, source_target_pairs={{0,28},{4,24},{8,20},{12,16},{16,12},{20,8},{24,4},{28,0},{1,29},{... | collective-permute-start | bytes 4915208 | tf_op jit(solution)/shard_map/ppermute | solution.py:102
  245.9 4.9 %collective-permute-start.10 = (f32[160,2048]{1,0:T(8,128)S(1)}, f32[160,2048]{1,0:T(8,128)S(1)}, u32[]{:S(2)}, u32[]{:S(2)}) collective-permute-start(f32[160,2048]{1,0:T(8,128)S(1)} %shard_map.42), channel_id=1, source_target_pairs={{0,1},{2,3},{4,5},{6,7},{9,8},{11,10},{13,12},{15,14},{16,17},{18,... | collective-permute-start | bytes 3932168 | tf_op jit(solution)/shard_map/ppermute | solution.py:117
  315.9 5.1 %collective-permute-start.13 = (f32[160,2048]{1,0:T(8,128)S(1)}, f32[160,2048]{1,0:T(8,128)}, u32[]{:S(2)}, u32[]{:S(2)}) collective-permute-start(f32[160,2048]{1,0:T(8,128)S(1)} %shard_map.43), channel_id=1, source_target_pairs={{0,1},{2,3},{4,5},{6,7},{9,8},{11,10},{13,12},{15,14},{16,17},{18,... | collective-permute-start | bytes 3932168 | tf_op jit(solution)/shard_map/ppermute | solution.py:117
  317.3 1.9 copy-start.4
  317.3 2.5 copy-start.5
  317.3 18.6 %collective-permute-start.11 = (f32[160,2048]{1,0:T(8,128)S(1)}, f32[160,2048]{1,0:T(8,128)S(1)}, u32[]{:S(2)}, u32[]{:S(2)}) collective-permute-start(f32[160,2048]{1,0:T(8,128)S(1)} %add.84), channel_id=1, source_target_pairs={{1,3},{5,7},{8,10},{12,14},{19,17},{23,21},{26,24},{30,28}} | collective-permute-start | bytes 3932168 | tf_op jit(solution)/shard_map/ppermute | solution.py:117
  322.4 27.6 %collective-permute-start.14 = (f32[160,2048]{1,0:T(8,128)S(1)}, f32[160,2048]{1,0:T(8,128)S(1)}, u32[]{:S(2)}, u32[]{:S(2)}) collective-permute-start(f32[160,2048]{1,0:T(8,128)S(1)} %add.88), channel_id=1, source_target_pairs={{1,3},{5,7},{8,10},{12,14},{19,17},{23,21},{26,24},{30,28}} | collective-permute-start | bytes 3932168 | tf_op jit(solution)/shard_map/ppermute | solution.py:117
  350.3 1.5 copy-start.3

commit v2 on v1

--- a/solution.py
+++ b/solution.py
@@ -8,6 +8,8 @@
 from jax.sharding import PartitionSpec as P
 
 BLOCK = 512
+SHORT = 10
+TILE = 16
 LINK_SHARE = 64
 CUT = 80
 
@@ -90,11 +92,16 @@
     bits = [1 << k for k in range(top.bit_length() - 1)]
     whole = {mask: (mask, 0, columns) for mask in range(vv)}
     first = [whole[mask] for mask in [*range(half, half + quarter), *range(1, half)]]
-    second = [whole[mask] for mask in range(half + quarter, vv)]
+    short = max(columns // SHORT // TILE, 1) * TILE
+    cuts = [0, columns - short, columns]
+    third = [(vv - 1, one, two - one) for one, two in zip(cuts, cuts[1:])]
+    second = [whole[mask] for mask in range(half + quarter, vv - 1)]
     ready = {}
-    for some in (first[:quarter], [*first[quarter:], whole[0], *second]):
+    for some in (first[:quarter], [*first[quarter:], whole[0], *second, whole[vv - 1]]):
         ready.update(zip(some, cut(some, block_owner, me, blocks)))
     got = {whole[0]: ready[whole[0]]}
+    for part in third:
+        ready[part] = ready[whole[vv - 1]][part[1] : part[1] + part[2]]
 
     def fetch(parts, *before):
         sent = [ready[part] for part in parts]
@@ -139,12 +146,12 @@
         return lax.dynamic_update_slice(out, jnp.where(mine, x, lax.dynamic_slice(out, (row, 0), x.shape)), (row, 0))
 
     fetch(first)
-    fetch(second[:-1], *[got[part] for part in first[:quarter]])
-    middle = [got[part] for part in second[:-1]]
-    fetch(second[-1:], *middle)
+    fetch(second, *[got[part] for part in first[:quarter]])
+    middle = [got[part] for part in second]
+    fetch(third, *middle)
     near = []
     for j in range(top):
-        arrived = [got[part] for part in first[: quarter * (j + 1) // top]]
+        arrived = [got[part] for part in first[:quarter]]
         near.append(multiply([whole[mask] for mask in range(j * ratio, (j + 1) * ratio)], *arrived))
     early = {}
     for j in range(top, top + top // 2):
@@ -155,8 +162,8 @@
     near = near + lax.ppermute(near, ("vv", "oo"), pairs)
     early = outer(early)
     late, before = {}, []
-    for part in second:
-        if part == second[-1]:
+    for part in [*second, *third]:
+        if part == third[0]:
             before += [near, *early.values()]
         sums = inner({part: multiply([part], *before)})
         before = list(sums.values())

time: 353 us -> 350 us (level)
  waiting for transfers between devices: 235 us -> 216 us
  Pallas kernels: 68 us -> 77.7 us
  starting transfers between devices: 27.7 us -> 31.4 us
    ppermute x6 -> x8, waiting for transfers between devices: 29.7 us -> 17.7 us  [hop(): return lax.ppermute(x, ('vv', 'oo'), pairs)]
    pallas_call x5 -> x6, Pallas kernels: 56.7 us -> 66.4 us  [product(): pl.pallas_call(product_kernel, grid=(rows // block,), in_specs=[pl.BlockS...]
    ppermute x7 -> x8, waiting for transfers between devices: 169 us -> 162 us  [fetch(): got[part] = lax.ppermute(x, 'vv', [(i, i ^ part[0]) for i in range(vv)])]
    ppermute x6 -> x8, starting transfers between devices: 10.9 us -> 13.4 us  [hop(): return lax.ppermute(x, ('vv', 'oo'), pairs)]
    ppermute x7 -> x8, starting transfers between devices: 10.8 us -> 12.1 us  [fetch(): got[part] = lax.ppermute(x, 'vv', [(i, i ^ part[0]) for i in range(vv)])]
  transfers between devices with their start and end apart: 15 -> 18, of which waited for: 10 -> 12; matrix products, arithmetic and copies ran while one was open for 4% -> 5% of each run, Pallas kernels for 15% -> 18%
where the time goes in v2:
time: 350 us; the launch traced here: 346 us
  waiting for transfers between devices  216 us (62%)
  Pallas kernels  77.7 us (22%)
  starting transfers between devices  31.4 us (9%)
  other arithmetic  15.6 us (4%)
  local copies, waits for them, and re-layouts  4.58 us (1%)
    ppermute x8, waiting for transfers between devices, fetch(): got[part] = lax.ppermute(x, 'vv', [(i, i ^ part[0]) for i in range(vv)])  162 us
    pallas_call x6, Pallas kernels, product(): pl.pallas_call(product_kernel, grid=(rows // block,), in_specs=[pl.BlockS...  66.4 us
    ppermute x1, waiting for transfers between devices, local(): near = near + lax.ppermute(near, ('vv', 'oo'), pairs)  35.8 us
    ppermute x8, waiting for transfers between devices, hop(): return lax.ppermute(x, ('vv', 'oo'), pairs)  17.7 us
    ppermute x8, starting transfers between devices, hop(): return lax.ppermute(x, ('vv', 'oo'), pairs)  13.4 us
    ppermute x8, starting transfers between devices, fetch(): got[part] = lax.ppermute(x, 'vv', [(i, i ^ part[0]) for i in range(vv)])  12.1 us
    pallas_call x2, Pallas kernels, cut(): pl.pallas_call(cut_kernel, grid_spec=pltpu.PrefetchScalarGridSpec(num_sca...  11.3 us
  transfers between devices with their start and end apart: 18, of which 12 were waited for; matrix products, arithmetic and copies ran while one was open for 5% of the time, Pallas kernels for 18%

profile of v2, /device:TPU:17, one launch (start us, length us, event | category | flops | bytes accessed | tf_op | source)
XLA Modules:
  0.0 345.6 jit_solution(5766860751437217017)
XLA Ops:
  0.0 3.9 %shard_map.38 = (bf16[160,5120]{1,0:T(8,128)(2,1)}, bf16[160,5120]{1,0:T(8,128)(2,1)}) custom-call(s32[8]{0:T(128)} %owner.3, s32[1]{0:T(128)} %bitcast.me, bf16[8,160,5120]{2,1,0:T(8,128)(2,1)} %bitcast.3, bf16[8,160,5120]{2,1,0:T(8,128)(2,1)} %bitcast.4), custom_call_target="tpu_custom_call" | custom-call | bytes 6553600 | tf_op jit(solution)/shard_map/pallas_call | solution.py:27
  3.9 3.3 collective-permute-start.4
  7.2 7.4 %shard_map.37 = (bf16[160,5120]{1,0:T(8,128)(2,1)}, bf16[160,5120]{1,0:T(8,128)(2,1)}, bf16[160,5120]{1,0:T(8,128)(2,1)}, bf16[160,5120]{1,0:T(8,128)(2,1)}, bf1...) custom-call(s32[8]{0:T(128)} %owner.3, s32[1]{0:T(128)} %bitcast.me, bf16[8,160,5120]{2,1,0:T(8,128)(2,1)} %bitcast.5, ...), custom_call_target="tpu_custom_call" | custom-call | bytes 19660800 | tf_op jit(solution)/shard_map/pallas_call | solution.py:27
  17.3 92.0 %collective-permute-done.3.refs_0_ = bf16[160,5120]{1,0:T(8,128)(2,1)S(1)} collective-permute-done((bf16[160,5120]{1,0:T(8,128)(2,1)}, bf16[160,5120]{1,0:T(8,128)(2,1)S(1)}, u32[]{:S(2)}, u32[]{:S(2)}) %collective-permute-start.3) | collective-permute-done | bytes 1638432 | tf_op jit(solution)/shard_map/ppermute | solution.py:109
  109.3 35.1 %collective-permute-done.4.refs_1_ = bf16[160,5120]{1,0:T(8,128)(2,1)S(1)} collective-permute-done((bf16[160,5120]{1,0:T(8,128)(2,1)}, bf16[160,5120]{1,0:T(8,128)(2,1)S(1)}, u32[]{:S(2)}, u32[]{:S(2)}) %collective-permute-start.4) | collective-permute-done | bytes 1638432 | tf_op jit(solution)/shard_map/ppermute | solution.py:109
  145.7 3.1 collective-permute-start.7
  148.8 1.4 copy-done.2
  150.2 11.6 %shard_map.39 = f32[320,2048]{1,0:T(8,128)S(1)} custom-call(bf16[160,5120]{1,0:T(8,128)(2,1)S(1)} %copy-done.2, bf16[160,5120]{1,0:T(8,128)(2,1)} %collective-permute-done.2.refs_1_, bf16[2048,5120]{1,0:T(8,128)(2,1)} %refs_1_.5), custom_call_target="tpu_custom_call" | custom-call | flops 104857600 | bytes 419840 | tf_op jit(solution)/shard_map/pallas_call | solution.py:61
  161.8 28.6 %collective-permute-done.1.refs_1_ = bf16[160,5120]{1,0:T(8,128)(2,1)} collective-permute-done((bf16[160,5120]{1,0:T(8,128)(2,1)}, bf16[160,5120]{1,0:T(8,128)(2,1)}, u32[]{:S(2)}, u32[]{:S(2)}) %collective-permute-start.1) | collective-permute-done | bytes 1638432 | tf_op jit(solution)/shard_map/ppermute | solution.py:109
  190.4 12.1 %shard_map.40 = f32[320,2048]{1,0:T(8,128)S(1)} custom-call(bf16[160,5120]{1,0:T(8,128)(2,1)} %collective-permute-done.refs_0_, bf16[160,5120]{1,0:T(8,128)(2,1)} %collective-permute-done.1.refs_1_, bf16[2048,5120]{1,0:T(8,128)(2,1)} %refs_1_.5), custom_call_target="tpu_custom_call" | custom-call | flops 104857600 | bytes 419840 | tf_op jit(solution)/shard_map/pallas_call | solution.py:61
  203.0 2.5 collective-permute-start.5
  205.5 11.1 %shard_map.41 = f32[320,2048]{1,0:T(8,128)S(1)} custom-call(bf16[160,5120]{1,0:T(8,128)(2,1)S(1)} %collective-permute-done.3.refs_0_, bf16[160,5120]{1,0:T(8,128)(2,1)S(1)} %copy-done.1, bf16[2048,5120]{1,0:T(8,128)(2,1)} %refs_1_.5), custom_call_target="tpu_custom_call" | custom-call | flops 104857600 | bytes 419840 | tf_op jit(solution)/shard_map/pallas_call | solution.py:61
  216.7 3.2 collective-permute-done.7.refs_0_
  219.8 3.1 collective-permute-start.8
  222.9 4.1 %select_add_fusion = f32[320,2048]{1,0:T(8,128)} fusion(f32[320,2048]{1,0:T(8,128)} %collective-permute-done.5, f32[320,2048]{1,0:T(8,128)S(1)} %shard_map.40, f32[320,2048]{1,0:T(8,128)S(1)} %shard_map.39, pred[]{:T(512)S(6)} %eq.21), kind=kLoop, calls=%fused_computation | loop fusion | flops 1310720 | bytes 10485761 | tf_op jit(solution)/shard_map/add | solution.py:141
  227.1 3.4 collective-permute-start.6
  231.0 2.2 collective-permute-start.9
  233.4 1.8 collective-permute-start.12
  235.2 10.9 %shard_map.42 = f32[160,2048]{1,0:T(8,128)S(1)} custom-call(bf16[160,5120]{1,0:T(8,128)(2,1)S(1)} %collective-permute-done.7.refs_0_, bf16[2048,5120]{1,0:T(8,128)(2,1)} %refs_1_.5), custom_call_target="tpu_custom_call" | custom-call | flops 52428800 | bytes 373760 | tf_op jit(solution)/shard_map/pallas_call | solution.py:61
  246.1 1.5 collective-permute-start.10
  247.6 3.4 collective-permute-done.10
  251.2 35.8 %collective-permute-done.6 = f32[320,2048]{1,0:T(8,128)S(1)} collective-permute-done((f32[320,2048]{1,0:T(8,128)}, f32[320,2048]{1,0:T(8,128)S(1)}, u32[]{:S(2)}, u32[]{:S(2)}) %collective-permute-start.6) | collective-permute-done | bytes 2621472 | tf_op jit(solution)/shard_map/ppermute | solution.py:162
  287.0 3.7 %add.89 = f32[320,2048]{1,0:T(8,128)} add(f32[320,2048]{1,0:T(8,128)} %select_add_fusion, f32[320,2048]{1,0:T(8,128)S(1)} %collective-permute-done.6) | non-fusion elementwise | flops 655360 | bytes 7864320 | tf_op jit(solution)/shard_map/add | solution.py:162
  290.7 3.7 %add.93 = f32[320,2048]{1,0:T(8,128)} add(f32[320,2048]{1,0:T(8,128)S(1)} %add.92, f32[320,2048]{1,0:T(8,128)} %collective-permute-done.9) | non-fusion elementwise | flops 655360 | bytes 7864320 | tf_op jit(solution)/shard_map/add | solution.py:133
  294.5 3.6 %collective-permute-done.12.refs_0_ = bf16[144,5120]{1,0:T(8,128)(2,1)S(1)} collective-permute-done((bf16[144,5120]{1,0:T(8,128)(2,1)S(1)}, bf16[144,5120]{1,0:T(8,128)(2,1)S(1)}, u32[]{:S(2)}, u32[]{:S(2)}) %collective-permute-start.12) | collective-permute-done | bytes 1474592 | tf_op jit(solution)/shard_map/ppermute | solution.py:109
  298.0 10.9 %shard_map.43 = f32[144,2048]{1,0:T(8,128)S(1)} custom-call(bf16[144,5120]{1,0:T(8,128)(2,1)S(1)} %collective-permute-done.12.refs_0_, bf16[2048,5120]{1,0:T(8,128)(2,1)} %refs_1_.5), custom_call_target="tpu_custom_call" | custom-call | flops 47185920 | bytes 369152 | tf_op jit(solution)/shard_map/pallas_call | solution.py:61
  311.6 1.4 collective-permute-start.11
  313.8 1.4 add.104
  317.0 9.7 %shard_map.44 = f32[16,2048]{1,0:T(8,128)S(1)} custom-call(bf16[16,5120]{1,0:T(8,128)(2,1)S(1)} %collective-permute-done.15.refs_0_, bf16[2048,5120]{1,0:T(8,128)(2,1)} %refs_1_.5), custom_call_target="tpu_custom_call" | custom-call | flops 5242880 | bytes 332288 | tf_op jit(solution)/shard_map/pallas_call | solution.py:61
  328.1 2.0 collective-permute-done.11
  331.8 10.9 %collective-permute-done.14 = f32[144,2048]{1,0:T(8,128)S(1)} collective-permute-done((f32[144,2048]{1,0:T(8,128)S(1)}, f32[144,2048]{1,0:T(8,128)S(1)}, u32[]{:S(2)}, u32[]{:S(2)}) %collective-permute-start.14) | collective-permute-done | bytes 1179680 | tf_op jit(solution)/shard_map/ppermute | solution.py:124
  344.1 1.5 copy-done.3
  (44 shorter events, 14.7 us)
Async XLA Ops:
  3.9 105.4 %collective-permute-start.3 = (bf16[160,5120]{1,0:T(8,128)(2,1)}, bf16[160,5120]{1,0:T(8,128)(2,1)S(1)}, u32[]{:S(2)}, u32[]{:S(2)}) collective-permute-start(bf16[160,5120]{1,0:T(8,128)(2,1)} %get-tuple-element.30), channel_id=1, source_target_pairs={{0,16},{4,20},{8,24},{12,28},{16,0},{20,4},{24,8},{28,12},{1,17},{... | collective-permute-start | bytes 4915208 | tf_op jit(solution)/shard_map/ppermute | solution.py:109
  3.9 140.5 %collective-permute-start.4 = (bf16[160,5120]{1,0:T(8,128)(2,1)}, bf16[160,5120]{1,0:T(8,128)(2,1)S(1)}, u32[]{:S(2)}, u32[]{:S(2)}) collective-permute-start(bf16[160,5120]{1,0:T(8,128)(2,1)} %get-tuple-element.31), channel_id=1, source_target_pairs={{0,20},{4,16},{8,28},{12,24},{16,4},{20,0},{24,12},{28,8},{1,21},{... | collective-permute-start | bytes 4915208 | tf_op jit(solution)/shard_map/ppermute | solution.py:109
  14.6 134.2 %collective-permute-start.2 = (bf16[160,5120]{1,0:T(8,128)(2,1)}, bf16[160,5120]{1,0:T(8,128)(2,1)}, u32[]{:S(2)}, u32[]{:S(2)}) collective-permute-start(bf16[160,5120]{1,0:T(8,128)(2,1)} %get-tuple-element.29), channel_id=1, source_target_pairs={{0,4},{4,0},{8,12},{12,8},{16,20},{20,16},{24,28},{28,24},{1,5},{5... | collective-permute-start | bytes 4915208 | tf_op jit(solution)/shard_map/ppermute | solution.py:109
  14.9 146.9 %collective-permute-start = (bf16[160,5120]{1,0:T(8,128)(2,1)}, bf16[160,5120]{1,0:T(8,128)(2,1)}, u32[]{:S(2)}, u32[]{:S(2)}) collective-permute-start(bf16[160,5120]{1,0:T(8,128)(2,1)} %get-tuple-element.26), channel_id=1, source_target_pairs={{0,8},{4,12},{8,0},{12,4},{16,24},{20,28},{24,16},{28,20},{1,9},{5... | collective-permute-start | bytes 4915208 | tf_op jit(solution)/shard_map/ppermute | solution.py:109
  16.2 174.2 %collective-permute-start.1 = (bf16[160,5120]{1,0:T(8,128)(2,1)}, bf16[160,5120]{1,0:T(8,128)(2,1)}, u32[]{:S(2)}, u32[]{:S(2)}) collective-permute-start(bf16[160,5120]{1,0:T(8,128)(2,1)} %get-tuple-element.27), channel_id=1, source_target_pairs={{0,12},{4,8},{8,4},{12,0},{16,28},{20,24},{24,20},{28,16},{1,13},{... | collective-permute-start | bytes 4915208 | tf_op jit(solution)/shard_map/ppermute | solution.py:109
  144.4 1.2 copy-start
  145.7 74.1 %collective-permute-start.7 = (bf16[160,5120]{1,0:T(8,128)(2,1)}, bf16[160,5120]{1,0:T(8,128)(2,1)S(1)}, u32[]{:S(2)}, u32[]{:S(2)}) collective-permute-start(bf16[160,5120]{1,0:T(8,128)(2,1)} %get-tuple-element.39), channel_id=1, source_target_pairs={{0,24},{4,28},{8,16},{12,20},{16,8},{20,12},{24,0},{28,4},{1,25},{... | collective-permute-start | bytes 4915208 | tf_op jit(solution)/shard_map/ppermute | solution.py:109
  148.8 1.4 copy-start.2
  202.5 3.0 copy-start.1
  203.0 19.9 %collective-permute-start.5 = (f32[320,2048]{1,0:T(8,128)S(1)}, f32[320,2048]{1,0:T(8,128)}, u32[]{:S(2)}, u32[]{:S(2)}) collective-permute-start(f32[320,2048]{1,0:T(8,128)S(1)} %broadcast_select_fusion), channel_id=1, source_target_pairs={{0,1},{1,0},{2,3},{3,2},{4,5},{5,4},{6,7},{7,6},{8,9},{9,8},{10,11... | collective-permute-start | bytes 7864328 | tf_op jit(solution)/shard_map/ppermute | solution.py:140
  219.8 10.7 %collective-permute-start.8 = (f32[320,2048]{1,0:T(8,128)S(1)}, f32[320,2048]{1,0:T(8,128)S(1)}, u32[]{:S(2)}, u32[]{:S(2)}) collective-permute-start(f32[320,2048]{1,0:T(8,128)S(1)} %shard_map.41), channel_id=1, source_target_pairs={{1,0},{3,2},{5,4},{7,6},{8,9},{10,11},{12,13},{14,15},{17,16},{19,... | collective-permute-start | bytes 7864328 | tf_op jit(solution)/shard_map/ppermute | solution.py:124
  227.1 6.2 %copy-start.6 = (bf16[160,5120]{1,0:T(8,128)(2,1)S(1)}, bf16[160,5120]{1,0:T(8,128)(2,1)}, u32[]{:S(2)}) copy-start(bf16[160,5120]{1,0:T(8,128)(2,1)} %get-tuple-element.42) | copy-start | bytes 4915204
  227.1 59.9 %collective-permute-start.6 = (f32[320,2048]{1,0:T(8,128)}, f32[320,2048]{1,0:T(8,128)S(1)}, u32[]{:S(2)}, u32[]{:S(2)}) collective-permute-start(f32[320,2048]{1,0:T(8,128)} %select_add_fusion), channel_id=1, source_target_pairs={{2,0},{3,1},{6,4},{7,5},{10,8},{11,9},{14,12},{15,13},{16,18},{17,... | collective-permute-start | bytes 7864328 | tf_op jit(solution)/shard_map/ppermute | solution.py:162
  231.0 59.7 %collective-permute-start.9 = (f32[320,2048]{1,0:T(8,128)S(1)}, f32[320,2048]{1,0:T(8,128)}, u32[]{:S(2)}, u32[]{:S(2)}) collective-permute-start(f32[320,2048]{1,0:T(8,128)S(1)} %add.92), channel_id=1, source_target_pairs={{0,2},{4,6},{9,11},{13,15},{18,16},{22,20},{27,25},{31,29}} | collective-permute-start | bytes 7864328 | tf_op jit(solution)/shard_map/ppermute | solution.py:124
  233.4 64.7 %collective-permute-start.12 = (bf16[144,5120]{1,0:T(8,128)(2,1)S(1)}, bf16[144,5120]{1,0:T(8,128)(2,1)S(1)}, u32[]{:S(2)}, u32[]{:S(2)}) collective-permute-start(bf16[144,5120]{1,0:T(8,128)(2,1)S(1)} %slice.22), channel_id=1, source_target_pairs={{0,28},{4,24},{8,20},{12,16},{16,12},{20,8},{24,4},{28,0},{1,29},{... | collective-permute-start | bytes 4423688 | tf_op jit(solution)/shard_map/ppermute | solution.py:109
  246.1 4.9 %collective-permute-start.10 = (f32[160,2048]{1,0:T(8,128)S(1)}, f32[160,2048]{1,0:T(8,128)S(1)}, u32[]{:S(2)}, u32[]{:S(2)}) collective-permute-start(f32[160,2048]{1,0:T(8,128)S(1)} %shard_map.42), channel_id=1, source_target_pairs={{0,1},{2,3},{4,5},{6,7},{9,8},{11,10},{13,12},{15,14},{16,17},{18,... | collective-permute-start | bytes 3932168 | tf_op jit(solution)/shard_map/ppermute | solution.py:124
  309.0 4.9 %collective-permute-start.13 = (f32[144,2048]{1,0:T(8,128)S(1)}, f32[144,2048]{1,0:T(8,128)}, u32[]{:S(2)}, u32[]{:S(2)}) collective-permute-start(f32[144,2048]{1,0:T(8,128)S(1)} %shard_map.43), channel_id=1, source_target_pairs={{0,1},{2,3},{4,5},{6,7},{9,8},{11,10},{13,12},{15,14},{16,17},{18,... | collective-permute-start | bytes 3538952 | tf_op jit(solution)/shard_map/ppermute | solution.py:124
  310.4 2.9 copy-start.4
  310.4 3.0 copy-start.5
  310.4 6.6 %collective-permute-start.15 = (bf16[16,5120]{1,0:T(8,128)(2,1)S(1)}, bf16[16,5120]{1,0:T(8,128)(2,1)S(1)}, u32[]{:S(2)}, u32[]{:S(2)}) collective-permute-start(bf16[16,5120]{1,0:T(8,128)(2,1)S(1)} %slice.23), channel_id=1, source_target_pairs={{0,28},{4,24},{8,20},{12,16},{16,12},{20,8},{24,4},{28,0},{1,29},{... | collective-permute-start | bytes 491528 | tf_op jit(solution)/shard_map/ppermute | solution.py:109
  311.6 18.5 %collective-permute-start.11 = (f32[160,2048]{1,0:T(8,128)S(1)}, f32[160,2048]{1,0:T(8,128)S(1)}, u32[]{:S(2)}, u32[]{:S(2)}) collective-permute-start(f32[160,2048]{1,0:T(8,128)S(1)} %add.100), channel_id=1, source_target_pairs={{1,3},{5,7},{8,10},{12,14},{19,17},{23,21},{26,24},{30,28}} | collective-permute-start | bytes 3932168 | tf_op jit(solution)/shard_map/ppermute | solution.py:124
  315.2 27.4 %collective-permute-start.14 = (f32[144,2048]{1,0:T(8,128)S(1)}, f32[144,2048]{1,0:T(8,128)S(1)}, u32[]{:S(2)}, u32[]{:S(2)}) collective-permute-start(f32[144,2048]{1,0:T(8,128)S(1)} %add.104), channel_id=1, source_target_pairs={{1,3},{5,7},{8,10},{12,14},{19,17},{23,21},{26,24},{30,28}} | collective-permute-start | bytes 3538952 | tf_op jit(solution)/shard_map/ppermute | solution.py:124
  326.7 3.7 %collective-permute-start.16 = (f32[16,2048]{1,0:T(8,128)S(1)}, f32[16,2048]{1,0:T(8,128)S(1)}, u32[]{:S(2)}, u32[]{:S(2)}) collective-permute-start(f32[16,2048]{1,0:T(8,128)S(1)} %shard_map.44), channel_id=1, source_target_pairs={{0,1},{2,3},{4,5},{6,7},{9,8},{11,10},{13,12},{15,14},{16,17},{18,... | collective-permute-start | bytes 393224 | tf_op jit(solution)/shard_map/ppermute | solution.py:124
  330.5 13.6 %collective-permute-start.17 = (f32[16,2048]{1,0:T(8,128)S(1)}, f32[16,2048]{1,0:T(8,128)S(1)}, u32[]{:S(2)}, u32[]{:S(2)}) collective-permute-start(f32[16,2048]{1,0:T(8,128)S(1)} %add.108), channel_id=1, source_target_pairs={{1,3},{5,7},{8,10},{12,14},{19,17},{23,21},{26,24},{30,28}} | collective-permute-start | bytes 393224 | tf_op jit(solution)/shard_map/ppermute | solution.py:124
  344.1 1.5 copy-start.3

commit v3 on v2

--- a/solution.py
+++ b/solution.py
@@ -165,6 +165,8 @@
     for part in [*second, *third]:
         if part == third[0]:
             before += [near, *early.values()]
+        if part == third[-1]:
+            before += [late[done] for done in second]
         sums = inner({part: multiply([part], *before)})
         before = list(sums.values())
         late.update(outer(sums))

time: 350 us -> 347 us (level); the launches traced: 346 us -> 346 us
  waiting for transfers between devices: 216 us -> 212 us
    ppermute x8, waiting for transfers between devices: 162 us -> 171 us  [fetch(): got[part] = lax.ppermute(x, 'vv', [(i, i ^ part[0]) for i in range(vv)])]
    ppermute x8, waiting for transfers between devices: 17.7 us -> 10.8 us  [hop(): return lax.ppermute(x, ('vv', 'oo'), pairs)]
    ppermute x1, waiting for transfers between devices: 35.8 us -> 30.4 us  [local(): near = near + lax.ppermute(near, ('vv', 'oo'), pairs)]
  transfers between devices with their start and end apart: 18 -> 18, of which waited for: 12 -> 11; matrix products, arithmetic and copies ran while one was open for 5% -> 5% of each run, Pallas kernels for 18% -> 21%
where the time goes in v3:
time: 347 us; the launch traced here: 346 us
  waiting for transfers between devices  212 us (61%)
  Pallas kernels  78.1 us (23%)
  starting transfers between devices  32.1 us (9%)
  other arithmetic  17 us (5%)
  local copies, waits for them, and re-layouts  6.88 us (2%)
    ppermute x8, waiting for transfers between devices, fetch(): got[part] = lax.ppermute(x, 'vv', [(i, i ^ part[0]) for i in range(vv)])  171 us
    pallas_call x6, Pallas kernels, product(): pl.pallas_call(product_kernel, grid=(rows // block,), in_specs=[pl.BlockS...  66.8 us
    ppermute x1, waiting for transfers between devices, local(): near = near + lax.ppermute(near, ('vv', 'oo'), pairs)  30.4 us
    ppermute x8, starting transfers between devices, hop(): return lax.ppermute(x, ('vv', 'oo'), pairs)  13.2 us
    ppermute x8, starting transfers between devices, fetch(): got[part] = lax.ppermute(x, 'vv', [(i, i ^ part[0]) for i in range(vv)])  11.7 us
    pallas_call x2, Pallas kernels, cut(): pl.pallas_call(cut_kernel, grid_spec=pltpu.PrefetchScalarGridSpec(num_sca...  11.3 us
    ppermute x8, waiting for transfers between devices, hop(): return lax.ppermute(x, ('vv', 'oo'), pairs)  10.8 us
  transfers between devices with their start and end apart: 18, of which 11 were waited for; matrix products, arithmetic and copies ran while one was open for 5% of the time, Pallas kernels for 21%

profile of v3, /device:TPU:17, one launch (start us, length us, event | category | flops | bytes accessed | tf_op | source)
XLA Modules:
  0.0 346.3 jit_solution(3586070729024079360)
XLA Ops:
  0.0 3.9 %shard_map.38 = (bf16[160,5120]{1,0:T(8,128)(2,1)}, bf16[160,5120]{1,0:T(8,128)(2,1)}) custom-call(s32[8]{0:T(128)} %owner.3, s32[1]{0:T(128)} %bitcast.me, bf16[8,160,5120]{2,1,0:T(8,128)(2,1)} %bitcast.3, bf16[8,160,5120]{2,1,0:T(8,128)(2,1)} %bitcast.4), custom_call_target="tpu_custom_call" | custom-call | bytes 6553600 | tf_op jit(solution)/shard_map/pallas_call | solution.py:27
  3.9 3.3 collective-permute-start.4
  7.2 7.4 %shard_map.37 = (bf16[160,5120]{1,0:T(8,128)(2,1)}, bf16[160,5120]{1,0:T(8,128)(2,1)}, bf16[160,5120]{1,0:T(8,128)(2,1)}, bf16[160,5120]{1,0:T(8,128)(2,1)}, bf1...) custom-call(s32[8]{0:T(128)} %owner.3, s32[1]{0:T(128)} %bitcast.me, bf16[8,160,5120]{2,1,0:T(8,128)(2,1)} %bitcast.5, ...), custom_call_target="tpu_custom_call" | custom-call | bytes 19660800 | tf_op jit(solution)/shard_map/pallas_call | solution.py:27
  17.3 92.0 %collective-permute-done.3.refs_0_ = bf16[160,5120]{1,0:T(8,128)(2,1)S(1)} collective-permute-done((bf16[160,5120]{1,0:T(8,128)(2,1)}, bf16[160,5120]{1,0:T(8,128)(2,1)S(1)}, u32[]{:S(2)}, u32[]{:S(2)}) %collective-permute-start.3) | collective-permute-done | bytes 1638432 | tf_op jit(solution)/shard_map/ppermute | solution.py:109
  110.5 33.9 %collective-permute-done.4.refs_1_ = bf16[160,5120]{1,0:T(8,128)(2,1)S(1)} collective-permute-done((bf16[160,5120]{1,0:T(8,128)(2,1)}, bf16[160,5120]{1,0:T(8,128)(2,1)S(1)}, u32[]{:S(2)}, u32[]{:S(2)}) %collective-permute-start.4) | collective-permute-done | bytes 1638432 | tf_op jit(solution)/shard_map/ppermute | solution.py:109
  145.7 3.1 collective-permute-start.7
  150.2 11.6 %shard_map.39 = f32[320,2048]{1,0:T(8,128)S(1)} custom-call(bf16[160,5120]{1,0:T(8,128)(2,1)S(1)} %copy-done.4, bf16[160,5120]{1,0:T(8,128)(2,1)} %collective-permute-done.2.refs_1_, bf16[2048,5120]{1,0:T(8,128)(2,1)} %refs_1_.5), custom_call_target="tpu_custom_call" | custom-call | flops 104857600 | bytes 419840 | tf_op jit(solution)/shard_map/pallas_call | solution.py:61
  161.8 28.6 %collective-permute-done.1.refs_1_ = bf16[160,5120]{1,0:T(8,128)(2,1)} collective-permute-done((bf16[160,5120]{1,0:T(8,128)(2,1)}, bf16[160,5120]{1,0:T(8,128)(2,1)}, u32[]{:S(2)}, u32[]{:S(2)}) %collective-permute-start.1) | collective-permute-done | bytes 1638432 | tf_op jit(solution)/shard_map/ppermute | solution.py:109
  190.4 12.1 %shard_map.40 = f32[320,2048]{1,0:T(8,128)S(1)} custom-call(bf16[160,5120]{1,0:T(8,128)(2,1)} %collective-permute-done.refs_0_, bf16[160,5120]{1,0:T(8,128)(2,1)} %collective-permute-done.1.refs_1_, bf16[2048,5120]{1,0:T(8,128)(2,1)} %refs_1_.5), custom_call_target="tpu_custom_call" | custom-call | flops 104857600 | bytes 419840 | tf_op jit(solution)/shard_map/pallas_call | solution.py:61
  203.0 2.5 collective-permute-start.5
  205.6 11.1 %shard_map.41 = f32[320,2048]{1,0:T(8,128)S(1)} custom-call(bf16[160,5120]{1,0:T(8,128)(2,1)S(1)} %copy-done.1, bf16[160,5120]{1,0:T(8,128)(2,1)S(1)} %copy-done.3, bf16[2048,5120]{1,0:T(8,128)(2,1)} %refs_1_.5), custom_call_target="tpu_custom_call" | custom-call | flops 104857600 | bytes 419840 | tf_op jit(solution)/shard_map/pallas_call | solution.py:61
  216.7 3.1 collective-permute-done.7.refs_0_
  219.8 3.1 collective-permute-start.8
  222.9 4.1 %select_add_fusion = f32[320,2048]{1,0:T(8,128)} fusion(f32[320,2048]{1,0:T(8,128)} %collective-permute-done.5, f32[320,2048]{1,0:T(8,128)S(1)} %shard_map.40, f32[320,2048]{1,0:T(8,128)S(1)} %shard_map.39, pred[]{:T(512)S(6)} %eq.21), kind=kLoop, calls=%fused_computation | loop fusion | flops 1310720 | bytes 10485761 | tf_op jit(solution)/shard_map/add | solution.py:141
  227.1 4.7 %collective-permute-start.6 = (f32[320,2048]{1,0:T(8,128)}, f32[320,2048]{1,0:T(8,128)}, u32[]{:S(2)}, u32[]{:S(2)}) collective-permute-start(f32[320,2048]{1,0:T(8,128)} %select_add_fusion), channel_id=1, source_target_pairs={{2,0},{3,1},{6,4},{7,5},{10,8},{11,9},{14,12},{15,13},{16,18},{17,... | collective-permute-start | bytes 7864328 | tf_op jit(solution)/shard_map/ppermute | solution.py:162
  231.8 2.0 add.92
  233.8 2.2 collective-permute-start.9
  237.3 1.8 collective-permute-start.12
  239.1 10.9 %shard_map.42 = f32[160,2048]{1,0:T(8,128)S(1)} custom-call(bf16[160,5120]{1,0:T(8,128)(2,1)S(1)} %collective-permute-done.7.refs_0_, bf16[2048,5120]{1,0:T(8,128)(2,1)} %refs_1_.5), custom_call_target="tpu_custom_call" | custom-call | flops 52428800 | bytes 373760 | tf_op jit(solution)/shard_map/pallas_call | solution.py:61
  252.2 2.7 collective-permute-done.10
  255.1 1.5 collective-permute-start.11
  256.6 30.4 %collective-permute-done.6 = f32[320,2048]{1,0:T(8,128)} collective-permute-done((f32[320,2048]{1,0:T(8,128)}, f32[320,2048]{1,0:T(8,128)}, u32[]{:S(2)}, u32[]{:S(2)}) %collective-permute-start.6) | collective-permute-done | bytes 2621472 | tf_op jit(solution)/shard_map/ppermute | solution.py:162
  287.0 3.0 add.89
  290.0 3.0 add.93
  293.0 12.8 %collective-permute-done.12.refs_0_ = bf16[144,5120]{1,0:T(8,128)(2,1)} collective-permute-done((bf16[144,5120]{1,0:T(8,128)(2,1)}, bf16[144,5120]{1,0:T(8,128)(2,1)}, u32[]{:S(2)}, u32[]{:S(2)}) %collective-permute-start.12) | collective-permute-done | bytes 1474592 | tf_op jit(solution)/shard_map/ppermute | solution.py:109
  305.9 11.4 %shard_map.43 = f32[144,2048]{1,0:T(8,128)S(1)} custom-call(bf16[144,5120]{1,0:T(8,128)(2,1)} %collective-permute-done.12.refs_0_, bf16[2048,5120]{1,0:T(8,128)(2,1)} %refs_1_.5), custom_call_target="tpu_custom_call" | custom-call | flops 47185920 | bytes 369152 | tf_op jit(solution)/shard_map/pallas_call | solution.py:61
  319.4 2.6 collective-permute-done.13
  325.0 9.7 %shard_map.44 = f32[16,2048]{1,0:T(8,128)S(1)} custom-call(bf16[16,5120]{1,0:T(8,128)(2,1)S(1)} %collective-permute-done.15.refs_0_, bf16[2048,5120]{1,0:T(8,128)(2,1)} %refs_1_.5), custom_call_target="tpu_custom_call" | custom-call | flops 5242880 | bytes 332288 | tf_op jit(solution)/shard_map/pallas_call | solution.py:61
  336.1 1.9 collective-permute-done.16
  340.4 1.9 select_dynamic-update-slice_fusion.1
  342.3 2.5 collective-permute-done.17
  344.8 1.5 copy-done.5
  (44 shorter events, 19.4 us)
Async XLA Ops:
  3.9 105.4 %collective-permute-start.3 = (bf16[160,5120]{1,0:T(8,128)(2,1)}, bf16[160,5120]{1,0:T(8,128)(2,1)S(1)}, u32[]{:S(2)}, u32[]{:S(2)}) collective-permute-start(bf16[160,5120]{1,0:T(8,128)(2,1)} %get-tuple-element.30), channel_id=1, source_target_pairs={{0,16},{4,20},{8,24},{12,28},{16,0},{20,4},{24,8},{28,12},{1,17},{... | collective-permute-start | bytes 4915208 | tf_op jit(solution)/shard_map/ppermute | solution.py:109
  3.9 140.5 %collective-permute-start.4 = (bf16[160,5120]{1,0:T(8,128)(2,1)}, bf16[160,5120]{1,0:T(8,128)(2,1)S(1)}, u32[]{:S(2)}, u32[]{:S(2)}) collective-permute-start(bf16[160,5120]{1,0:T(8,128)(2,1)} %get-tuple-element.31), channel_id=1, source_target_pairs={{0,20},{4,16},{8,28},{12,24},{16,4},{20,0},{24,12},{28,8},{1,21},{... | collective-permute-start | bytes 4915208 | tf_op jit(solution)/shard_map/ppermute | solution.py:109
  14.6 134.2 %collective-permute-start.2 = (bf16[160,5120]{1,0:T(8,128)(2,1)}, bf16[160,5120]{1,0:T(8,128)(2,1)}, u32[]{:S(2)}, u32[]{:S(2)}) collective-permute-start(bf16[160,5120]{1,0:T(8,128)(2,1)} %get-tuple-element.29), channel_id=1, source_target_pairs={{0,4},{4,0},{8,12},{12,8},{16,20},{20,16},{24,28},{28,24},{1,5},{5... | collective-permute-start | bytes 4915208 | tf_op jit(solution)/shard_map/ppermute | solution.py:109
  14.9 146.9 %collective-permute-start = (bf16[160,5120]{1,0:T(8,128)(2,1)}, bf16[160,5120]{1,0:T(8,128)(2,1)}, u32[]{:S(2)}, u32[]{:S(2)}) collective-permute-start(bf16[160,5120]{1,0:T(8,128)(2,1)} %get-tuple-element.26), channel_id=1, source_target_pairs={{0,8},{4,12},{8,0},{12,4},{16,24},{20,28},{24,16},{28,20},{1,9},{5... | collective-permute-start | bytes 4915208 | tf_op jit(solution)/shard_map/ppermute | solution.py:109
  16.2 174.2 %collective-permute-start.1 = (bf16[160,5120]{1,0:T(8,128)(2,1)}, bf16[160,5120]{1,0:T(8,128)(2,1)}, u32[]{:S(2)}, u32[]{:S(2)}) collective-permute-start(bf16[160,5120]{1,0:T(8,128)(2,1)} %get-tuple-element.27), channel_id=1, source_target_pairs={{0,12},{4,8},{8,4},{12,0},{16,28},{20,24},{24,20},{28,16},{1,13},{... | collective-permute-start | bytes 4915208 | tf_op jit(solution)/shard_map/ppermute | solution.py:109
  109.3 1.2 copy-start
  144.4 1.2 copy-start.2
  145.7 74.1 %collective-permute-start.7 = (bf16[160,5120]{1,0:T(8,128)(2,1)}, bf16[160,5120]{1,0:T(8,128)(2,1)S(1)}, u32[]{:S(2)}, u32[]{:S(2)}) collective-permute-start(bf16[160,5120]{1,0:T(8,128)(2,1)} %get-tuple-element.39), channel_id=1, source_target_pairs={{0,24},{4,28},{8,16},{12,20},{16,8},{20,12},{24,0},{28,4},{1,25},{... | collective-permute-start | bytes 4915208 | tf_op jit(solution)/shard_map/ppermute | solution.py:109
  148.8 1.4 copy-start.4
  202.5 3.0 copy-start.1
  202.5 3.0 copy-start.3
  203.0 19.9 %collective-permute-start.5 = (f32[320,2048]{1,0:T(8,128)S(1)}, f32[320,2048]{1,0:T(8,128)}, u32[]{:S(2)}, u32[]{:S(2)}) collective-permute-start(f32[320,2048]{1,0:T(8,128)S(1)} %broadcast_select_fusion), channel_id=1, source_target_pairs={{0,1},{1,0},{2,3},{3,2},{4,5},{5,4},{6,7},{7,6},{8,9},{9,8},{10,11... | collective-permute-start | bytes 7864328 | tf_op jit(solution)/shard_map/ppermute | solution.py:140
  219.8 12.0 %collective-permute-start.8 = (f32[320,2048]{1,0:T(8,128)S(1)}, f32[320,2048]{1,0:T(8,128)S(1)}, u32[]{:S(2)}, u32[]{:S(2)}) collective-permute-start(f32[320,2048]{1,0:T(8,128)S(1)} %shard_map.41), channel_id=1, source_target_pairs={{1,0},{3,2},{5,4},{7,6},{8,9},{10,11},{12,13},{14,15},{17,16},{19,... | collective-permute-start | bytes 7864328 | tf_op jit(solution)/shard_map/ppermute | solution.py:124
  227.1 9.0 %copy-start.6 = (bf16[160,5120]{1,0:T(8,128)(2,1)S(1)}, bf16[160,5120]{1,0:T(8,128)(2,1)}, u32[]{:S(2)}) copy-start(bf16[160,5120]{1,0:T(8,128)(2,1)} %get-tuple-element.42) | copy-start | bytes 4915204
  227.1 59.9 %collective-permute-start.6 = (f32[320,2048]{1,0:T(8,128)}, f32[320,2048]{1,0:T(8,128)}, u32[]{:S(2)}, u32[]{:S(2)}) collective-permute-start(f32[320,2048]{1,0:T(8,128)} %select_add_fusion), channel_id=1, source_target_pairs={{2,0},{3,1},{6,4},{7,5},{10,8},{11,9},{14,12},{15,13},{16,18},{17,... | collective-permute-start | bytes 7864328 | tf_op jit(solution)/shard_map/ppermute | solution.py:162
  233.8 56.2 %collective-permute-start.9 = (f32[320,2048]{1,0:T(8,128)}, f32[320,2048]{1,0:T(8,128)}, u32[]{:S(2)}, u32[]{:S(2)}) collective-permute-start(f32[320,2048]{1,0:T(8,128)} %add.92), channel_id=1, source_target_pairs={{0,2},{4,6},{9,11},{13,15},{18,16},{22,20},{27,25},{31,29}} | collective-permute-start | bytes 7864328 | tf_op jit(solution)/shard_map/ppermute | solution.py:124
  237.3 68.6 %collective-permute-start.12 = (bf16[144,5120]{1,0:T(8,128)(2,1)}, bf16[144,5120]{1,0:T(8,128)(2,1)}, u32[]{:S(2)}, u32[]{:S(2)}) collective-permute-start(bf16[144,5120]{1,0:T(8,128)(2,1)} %slice.22), channel_id=1, source_target_pairs={{0,28},{4,24},{8,20},{12,16},{16,12},{20,8},{24,4},{28,0},{1,29},{... | collective-permute-start | bytes 4423688 | tf_op jit(solution)/shard_map/ppermute | solution.py:109
  250.0 4.9 %collective-permute-start.10 = (f32[160,2048]{1,0:T(8,128)S(1)}, f32[160,2048]{1,0:T(8,128)S(1)}, u32[]{:S(2)}, u32[]{:S(2)}) collective-permute-start(f32[160,2048]{1,0:T(8,128)S(1)} %shard_map.42), channel_id=1, source_target_pairs={{0,1},{2,3},{4,5},{6,7},{9,8},{11,10},{13,12},{15,14},{16,17},{18,... | collective-permute-start | bytes 3932168 | tf_op jit(solution)/shard_map/ppermute | solution.py:124
  251.4 73.6 %collective-permute-start.15 = (bf16[16,5120]{1,0:T(8,128)(2,1)S(1)}, bf16[16,5120]{1,0:T(8,128)(2,1)S(1)}, u32[]{:S(2)}, u32[]{:S(2)}) collective-permute-start(bf16[16,5120]{1,0:T(8,128)(2,1)S(1)} %slice.23), channel_id=1, source_target_pairs={{0,28},{4,24},{8,20},{12,16},{16,12},{20,8},{24,4},{28,0},{1,29},{... | collective-permute-start | bytes 491528 | tf_op jit(solution)/shard_map/ppermute | solution.py:109
  255.1 69.6 %collective-permute-start.11 = (f32[160,2048]{1,0:T(8,128)S(1)}, f32[160,2048]{1,0:T(8,128)S(1)}, u32[]{:S(2)}, u32[]{:S(2)}) collective-permute-start(f32[160,2048]{1,0:T(8,128)S(1)} %add.100), channel_id=1, source_target_pairs={{1,3},{5,7},{8,10},{12,14},{19,17},{23,21},{26,24},{30,28}} | collective-permute-start | bytes 3932168 | tf_op jit(solution)/shard_map/ppermute | solution.py:124
  317.3 4.7 %collective-permute-start.13 = (f32[144,2048]{1,0:T(8,128)S(1)}, f32[144,2048]{1,0:T(8,128)S(1)}, u32[]{:S(2)}, u32[]{:S(2)}) collective-permute-start(f32[144,2048]{1,0:T(8,128)S(1)} %shard_map.43), channel_id=1, source_target_pairs={{0,1},{2,3},{4,5},{6,7},{9,8},{11,10},{13,12},{15,14},{16,17},{18,... | collective-permute-start | bytes 3538952 | tf_op jit(solution)/shard_map/ppermute | solution.py:124
  323.2 17.3 %collective-permute-start.14 = (f32[144,2048]{1,0:T(8,128)}, f32[144,2048]{1,0:T(8,128)}, u32[]{:S(2)}, u32[]{:S(2)}) collective-permute-start(f32[144,2048]{1,0:T(8,128)} %add.104), channel_id=1, source_target_pairs={{1,3},{5,7},{8,10},{12,14},{19,17},{23,21},{26,24},{30,28}} | collective-permute-start | bytes 3538952 | tf_op jit(solution)/shard_map/ppermute | solution.py:124
  334.8 3.2 collective-permute-start.16
  338.0 6.8 %collective-permute-start.17 = (f32[16,2048]{1,0:T(8,128)S(1)}, f32[16,2048]{1,0:T(8,128)S(1)}, u32[]{:S(2)}, u32[]{:S(2)}) collective-permute-start(f32[16,2048]{1,0:T(8,128)S(1)} %add.108), channel_id=1, source_target_pairs={{1,3},{5,7},{8,10},{12,14},{19,17},{23,21},{26,24},{30,28}} | collective-permute-start | bytes 393224 | tf_op jit(solution)/shard_map/ppermute | solution.py:124
  344.8 1.5 copy-start.5

commit v4 on v2

--- a/solution.py
+++ b/solution.py
@@ -93,7 +93,7 @@
     whole = {mask: (mask, 0, columns) for mask in range(vv)}
     first = [whole[mask] for mask in [*range(half, half + quarter), *range(1, half)]]
     short = max(columns // SHORT // TILE, 1) * TILE
-    cuts = [0, columns - short, columns]
+    cuts = [0, short, columns]
     third = [(vv - 1, one, two - one) for one, two in zip(cuts, cuts[1:])]
     second = [whole[mask] for mask in range(half + quarter, vv - 1)]
     ready = {}

time: 350 us -> 357 us (1.020)
  waiting for transfers between devices: 216 us -> 229 us
    ppermute x8, waiting for transfers between devices: 162 us -> 173 us  [fetch(): got[part] = lax.ppermute(x, 'vv', [(i, i ^ part[0]) for i in range(vv)])]
  transfers between devices with their start and end apart: 18 -> 18, of which waited for: 12 -> 10; matrix products, arithmetic and copies ran while one was open for 5% -> 4% of each run, Pallas kernels for 18% -> 21%
where the time goes in v4:
time: 357 us; the launch traced here: 356 us
  waiting for transfers between devices  229 us (64%)
  Pallas kernels  77.8 us (22%)
  starting transfers between devices  30.6 us (9%)
  other arithmetic  12.8 us (4%)
  local copies, waits for them, and re-layouts  5.7 us (2%)
    ppermute x8, waiting for transfers between devices, fetch(): got[part] = lax.ppermute(x, 'vv', [(i, i ^ part[0]) for i in range(vv)])  173 us
    pallas_call x6, Pallas kernels, product(): pl.pallas_call(product_kernel, grid=(rows // block,), in_specs=[pl.BlockS...  66.5 us
    ppermute x1, waiting for transfers between devices, local(): near = near + lax.ppermute(near, ('vv', 'oo'), pairs)  36.1 us
    ppermute x8, waiting for transfers between devices, hop(): return lax.ppermute(x, ('vv', 'oo'), pairs)  19.9 us
    ppermute x8, starting transfers between devices, fetch(): got[part] = lax.ppermute(x, 'vv', [(i, i ^ part[0]) for i in range(vv)])  12.5 us
    ppermute x8, starting transfers between devices, hop(): return lax.ppermute(x, ('vv', 'oo'), pairs)  12.1 us
    pallas_call x2, Pallas kernels, cut(): pl.pallas_call(cut_kernel, grid_spec=pltpu.PrefetchScalarGridSpec(num_sca...  11.3 us
  transfers between devices with their start and end apart: 18, of which 10 were waited for; matrix products, arithmetic and copies ran while one was open for 4% of the time, Pallas kernels for 21%

profile of v4, /device:TPU:17, one launch (start us, length us, event | category | flops | bytes accessed | tf_op | source)
XLA Modules:
  0.0 355.9 jit_solution(7258851826619867835)
XLA Ops:
  0.0 3.9 %shard_map.38 = (bf16[160,5120]{1,0:T(8,128)(2,1)}, bf16[160,5120]{1,0:T(8,128)(2,1)}) custom-call(s32[8]{0:T(128)} %owner.3, s32[1]{0:T(128)} %bitcast.me, bf16[8,160,5120]{2,1,0:T(8,128)(2,1)} %bitcast.3, bf16[8,160,5120]{2,1,0:T(8,128)(2,1)} %bitcast.4), custom_call_target="tpu_custom_call" | custom-call | bytes 6553600 | tf_op jit(solution)/shard_map/pallas_call | solution.py:27
  3.9 3.3 collective-permute-start.4
  7.2 7.4 %shard_map.37 = (bf16[160,5120]{1,0:T(8,128)(2,1)}, bf16[160,5120]{1,0:T(8,128)(2,1)}, bf16[160,5120]{1,0:T(8,128)(2,1)}, bf16[160,5120]{1,0:T(8,128)(2,1)}, bf1...) custom-call(s32[8]{0:T(128)} %owner.3, s32[1]{0:T(128)} %bitcast.me, bf16[8,160,5120]{2,1,0:T(8,128)(2,1)} %bitcast.5, ...), custom_call_target="tpu_custom_call" | custom-call | bytes 19660800 | tf_op jit(solution)/shard_map/pallas_call | solution.py:27
  14.9 1.3 collective-permute-start
  17.3 92.0 %collective-permute-done.3.refs_0_ = bf16[160,5120]{1,0:T(8,128)(2,1)S(1)} collective-permute-done((bf16[160,5120]{1,0:T(8,128)(2,1)}, bf16[160,5120]{1,0:T(8,128)(2,1)S(1)}, u32[]{:S(2)}, u32[]{:S(2)}) %collective-permute-start.3) | collective-permute-done | bytes 1638432 | tf_op jit(solution)/shard_map/ppermute | solution.py:109
  109.3 35.1 %collective-permute-done.4.refs_1_ = bf16[160,5120]{1,0:T(8,128)(2,1)S(1)} collective-permute-done((bf16[160,5120]{1,0:T(8,128)(2,1)}, bf16[160,5120]{1,0:T(8,128)(2,1)S(1)}, u32[]{:S(2)}, u32[]{:S(2)}) %collective-permute-start.4) | collective-permute-done | bytes 1638432 | tf_op jit(solution)/shard_map/ppermute | solution.py:109
  145.7 3.1 collective-permute-start.7
  148.8 1.4 copy-done.2
  150.2 11.6 %shard_map.39 = f32[320,2048]{1,0:T(8,128)S(1)} custom-call(bf16[160,5120]{1,0:T(8,128)(2,1)S(1)} %copy-done.2, bf16[160,5120]{1,0:T(8,128)(2,1)} %collective-permute-done.2.refs_1_, bf16[2048,5120]{1,0:T(8,128)(2,1)} %refs_1_.5), custom_call_target="tpu_custom_call" | custom-call | flops 104857600 | bytes 419840 | tf_op jit(solution)/shard_map/pallas_call | solution.py:61
  161.8 28.6 %collective-permute-done.1.refs_1_ = bf16[160,5120]{1,0:T(8,128)(2,1)} collective-permute-done((bf16[160,5120]{1,0:T(8,128)(2,1)}, bf16[160,5120]{1,0:T(8,128)(2,1)}, u32[]{:S(2)}, u32[]{:S(2)}) %collective-permute-start.1) | collective-permute-done | bytes 1638432 | tf_op jit(solution)/shard_map/ppermute | solution.py:109
  190.4 12.1 %shard_map.40 = f32[320,2048]{1,0:T(8,128)S(1)} custom-call(bf16[160,5120]{1,0:T(8,128)(2,1)} %collective-permute-done.refs_0_, bf16[160,5120]{1,0:T(8,128)(2,1)} %collective-permute-done.1.refs_1_, bf16[2048,5120]{1,0:T(8,128)(2,1)} %refs_1_.5), custom_call_target="tpu_custom_call" | custom-call | flops 104857600 | bytes 419840 | tf_op jit(solution)/shard_map/pallas_call | solution.py:61
  203.0 2.5 collective-permute-start.5
  205.5 11.1 %shard_map.41 = f32[320,2048]{1,0:T(8,128)S(1)} custom-call(bf16[160,5120]{1,0:T(8,128)(2,1)S(1)} %collective-permute-done.3.refs_0_, bf16[160,5120]{1,0:T(8,128)(2,1)S(1)} %copy-done.1, bf16[2048,5120]{1,0:T(8,128)(2,1)} %refs_1_.5), custom_call_target="tpu_custom_call" | custom-call | flops 104857600 | bytes 419840 | tf_op jit(solution)/shard_map/pallas_call | solution.py:61
  216.7 3.2 collective-permute-done.7.refs_0_
  219.8 3.1 collective-permute-start.8
  222.9 4.1 %select_add_fusion = f32[320,2048]{1,0:T(8,128)} fusion(f32[320,2048]{1,0:T(8,128)} %collective-permute-done.5, f32[320,2048]{1,0:T(8,128)S(1)} %shard_map.40, f32[320,2048]{1,0:T(8,128)S(1)} %shard_map.39, pred[]{:T(512)S(6)} %eq.21), kind=kLoop, calls=%fused_computation | loop fusion | flops 1310720 | bytes 10485761 | tf_op jit(solution)/shard_map/add | solution.py:141
  227.1 3.4 collective-permute-start.6
  233.1 1.8 collective-permute-start.15
  234.9 10.9 %shard_map.42 = f32[160,2048]{1,0:T(8,128)S(1)} custom-call(bf16[160,5120]{1,0:T(8,128)(2,1)S(1)} %collective-permute-done.7.refs_0_, bf16[2048,5120]{1,0:T(8,128)(2,1)} %refs_1_.5), custom_call_target="tpu_custom_call" | custom-call | flops 52428800 | bytes 373760 | tf_op jit(solution)/shard_map/pallas_call | solution.py:61
  245.8 1.5 collective-permute-start.10
  247.3 1.6 collective-permute-start.12
  248.9 1.8 collective-permute-done.10
  250.9 36.1 %collective-permute-done.6 = f32[320,2048]{1,0:T(8,128)S(1)} collective-permute-done((f32[320,2048]{1,0:T(8,128)}, f32[320,2048]{1,0:T(8,128)S(1)}, u32[]{:S(2)}, u32[]{:S(2)}) %collective-permute-start.6) | collective-permute-done | bytes 2621472 | tf_op jit(solution)/shard_map/ppermute | solution.py:162
  287.0 3.7 %add.89 = f32[320,2048]{1,0:T(8,128)} add(f32[320,2048]{1,0:T(8,128)} %select_add_fusion, f32[320,2048]{1,0:T(8,128)S(1)} %collective-permute-done.6) | non-fusion elementwise | flops 655360 | bytes 7864320 | tf_op jit(solution)/shard_map/add | solution.py:162
  290.7 2.0 add.93
  292.7 13.7 %collective-permute-done.12.refs_0_ = bf16[16,5120]{1,0:T(8,128)(2,1)S(1)} collective-permute-done((bf16[16,5120]{1,0:T(8,128)(2,1)S(1)}, bf16[16,5120]{1,0:T(8,128)(2,1)S(1)}, u32[]{:S(2)}, u32[]{:S(2)}) %collective-permute-start.12) | collective-permute-done | bytes 163872 | tf_op jit(solution)/shard_map/ppermute | solution.py:109
  306.4 9.7 %shard_map.43 = f32[16,2048]{1,0:T(8,128)S(1)} custom-call(bf16[16,5120]{1,0:T(8,128)(2,1)S(1)} %collective-permute-done.12.refs_0_, bf16[2048,5120]{1,0:T(8,128)(2,1)} %refs_1_.5), custom_call_target="tpu_custom_call" | custom-call | flops 5242880 | bytes 332288 | tf_op jit(solution)/shard_map/pallas_call | solution.py:61
  319.4 11.1 %shard_map.44 = f32[144,2048]{1,0:T(8,128)S(1)} custom-call(bf16[144,5120]{1,0:T(8,128)(2,1)S(1)} %collective-permute-done.15.refs_0_, bf16[2048,5120]{1,0:T(8,128)(2,1)} %refs_1_.5), custom_call_target="tpu_custom_call" | custom-call | flops 47185920 | bytes 369152 | tf_op jit(solution)/shard_map/pallas_call | solution.py:61
  330.5 1.6 collective-permute-start.16
  333.1 2.5 collective-permute-done.16
  338.9 15.1 %collective-permute-done.14 = f32[16,2048]{1,0:T(8,128)S(1)} collective-permute-done((f32[16,2048]{1,0:T(8,128)S(1)}, f32[16,2048]{1,0:T(8,128)S(1)}, u32[]{:S(2)}, u32[]{:S(2)}) %collective-permute-start.14) | collective-permute-done | bytes 131104 | tf_op jit(solution)/shard_map/ppermute | solution.py:124
  354.4 1.5 copy-done.3
  (44 shorter events, 13.6 us)
Async XLA Ops:
  3.9 105.4 %collective-permute-start.3 = (bf16[160,5120]{1,0:T(8,128)(2,1)}, bf16[160,5120]{1,0:T(8,128)(2,1)S(1)}, u32[]{:S(2)}, u32[]{:S(2)}) collective-permute-start(bf16[160,5120]{1,0:T(8,128)(2,1)} %get-tuple-element.30), channel_id=1, source_target_pairs={{0,16},{4,20},{8,24},{12,28},{16,0},{20,4},{24,8},{28,12},{1,17},{... | collective-permute-start | bytes 4915208 | tf_op jit(solution)/shard_map/ppermute | solution.py:109
  3.9 140.5 %collective-permute-start.4 = (bf16[160,5120]{1,0:T(8,128)(2,1)}, bf16[160,5120]{1,0:T(8,128)(2,1)S(1)}, u32[]{:S(2)}, u32[]{:S(2)}) collective-permute-start(bf16[160,5120]{1,0:T(8,128)(2,1)} %get-tuple-element.31), channel_id=1, source_target_pairs={{0,20},{4,16},{8,28},{12,24},{16,4},{20,0},{24,12},{28,8},{1,21},{... | collective-permute-start | bytes 4915208 | tf_op jit(solution)/shard_map/ppermute | solution.py:109
  14.6 134.2 %collective-permute-start.2 = (bf16[160,5120]{1,0:T(8,128)(2,1)}, bf16[160,5120]{1,0:T(8,128)(2,1)}, u32[]{:S(2)}, u32[]{:S(2)}) collective-permute-start(bf16[160,5120]{1,0:T(8,128)(2,1)} %get-tuple-element.29), channel_id=1, source_target_pairs={{0,4},{4,0},{8,12},{12,8},{16,20},{20,16},{24,28},{28,24},{1,5},{5... | collective-permute-start | bytes 4915208 | tf_op jit(solution)/shard_map/ppermute | solution.py:109
  14.9 146.9 %collective-permute-start = (bf16[160,5120]{1,0:T(8,128)(2,1)}, bf16[160,5120]{1,0:T(8,128)(2,1)}, u32[]{:S(2)}, u32[]{:S(2)}) collective-permute-start(bf16[160,5120]{1,0:T(8,128)(2,1)} %get-tuple-element.26), channel_id=1, source_target_pairs={{0,8},{4,12},{8,0},{12,4},{16,24},{20,28},{24,16},{28,20},{1,9},{5... | collective-permute-start | bytes 4915208 | tf_op jit(solution)/shard_map/ppermute | solution.py:109
  16.2 174.2 %collective-permute-start.1 = (bf16[160,5120]{1,0:T(8,128)(2,1)}, bf16[160,5120]{1,0:T(8,128)(2,1)}, u32[]{:S(2)}, u32[]{:S(2)}) collective-permute-start(bf16[160,5120]{1,0:T(8,128)(2,1)} %get-tuple-element.27), channel_id=1, source_target_pairs={{0,12},{4,8},{8,4},{12,0},{16,28},{20,24},{24,20},{28,16},{1,13},{... | collective-permute-start | bytes 4915208 | tf_op jit(solution)/shard_map/ppermute | solution.py:109
  144.4 1.2 copy-start
  145.7 74.1 %collective-permute-start.7 = (bf16[160,5120]{1,0:T(8,128)(2,1)}, bf16[160,5120]{1,0:T(8,128)(2,1)S(1)}, u32[]{:S(2)}, u32[]{:S(2)}) collective-permute-start(bf16[160,5120]{1,0:T(8,128)(2,1)} %get-tuple-element.39), channel_id=1, source_target_pairs={{0,24},{4,28},{8,16},{12,20},{16,8},{20,12},{24,0},{28,4},{1,25},{... | collective-permute-start | bytes 4915208 | tf_op jit(solution)/shard_map/ppermute | solution.py:109
  148.8 1.4 copy-start.2
  202.5 3.0 copy-start.1
  203.0 19.9 %collective-permute-start.5 = (f32[320,2048]{1,0:T(8,128)S(1)}, f32[320,2048]{1,0:T(8,128)}, u32[]{:S(2)}, u32[]{:S(2)}) collective-permute-start(f32[320,2048]{1,0:T(8,128)S(1)} %broadcast_select_fusion), channel_id=1, source_target_pairs={{0,1},{1,0},{2,3},{3,2},{4,5},{5,4},{6,7},{7,6},{8,9},{9,8},{10,11... | collective-permute-start | bytes 7864328 | tf_op jit(solution)/shard_map/ppermute | solution.py:140
  219.8 10.7 %collective-permute-start.8 = (f32[320,2048]{1,0:T(8,128)S(1)}, f32[320,2048]{1,0:T(8,128)S(1)}, u32[]{:S(2)}, u32[]{:S(2)}) collective-permute-start(f32[320,2048]{1,0:T(8,128)S(1)} %shard_map.41), channel_id=1, source_target_pairs={{1,0},{3,2},{5,4},{7,6},{8,9},{10,11},{12,13},{14,15},{17,16},{19,... | collective-permute-start | bytes 7864328 | tf_op jit(solution)/shard_map/ppermute | solution.py:124
  227.1 4.8 %copy-start.6 = (bf16[160,5120]{1,0:T(8,128)(2,1)S(1)}, bf16[160,5120]{1,0:T(8,128)(2,1)}, u32[]{:S(2)}) copy-start(bf16[160,5120]{1,0:T(8,128)(2,1)} %get-tuple-element.42) | copy-start | bytes 4915204
  227.1 59.9 %collective-permute-start.6 = (f32[320,2048]{1,0:T(8,128)}, f32[320,2048]{1,0:T(8,128)S(1)}, u32[]{:S(2)}, u32[]{:S(2)}) collective-permute-start(f32[320,2048]{1,0:T(8,128)} %select_add_fusion), channel_id=1, source_target_pairs={{2,0},{3,1},{6,4},{7,5},{10,8},{11,9},{14,12},{15,13},{16,18},{17,... | collective-permute-start | bytes 7864328 | tf_op jit(solution)/shard_map/ppermute | solution.py:162
  231.0 59.7 %collective-permute-start.9 = (f32[320,2048]{1,0:T(8,128)S(1)}, f32[320,2048]{1,0:T(8,128)S(1)}, u32[]{:S(2)}, u32[]{:S(2)}) collective-permute-start(f32[320,2048]{1,0:T(8,128)S(1)} %add.92), channel_id=1, source_target_pairs={{0,2},{4,6},{9,11},{13,15},{18,16},{22,20},{27,25},{31,29}} | collective-permute-start | bytes 7864328 | tf_op jit(solution)/shard_map/ppermute | solution.py:124
  233.1 86.3 %collective-permute-start.15 = (bf16[144,5120]{1,0:T(8,128)(2,1)}, bf16[144,5120]{1,0:T(8,128)(2,1)S(1)}, u32[]{:S(2)}, u32[]{:S(2)}) collective-permute-start(bf16[144,5120]{1,0:T(8,128)(2,1)} %slice.23), channel_id=1, source_target_pairs={{0,28},{4,24},{8,20},{12,16},{16,12},{20,8},{24,4},{28,0},{1,29},{... | collective-permute-start | bytes 4423688 | tf_op jit(solution)/shard_map/ppermute | solution.py:109
  245.8 4.9 %collective-permute-start.10 = (f32[160,2048]{1,0:T(8,128)S(1)}, f32[160,2048]{1,0:T(8,128)S(1)}, u32[]{:S(2)}, u32[]{:S(2)}) collective-permute-start(f32[160,2048]{1,0:T(8,128)S(1)} %shard_map.42), channel_id=1, source_target_pairs={{0,1},{2,3},{4,5},{6,7},{9,8},{11,10},{13,12},{15,14},{16,17},{18,... | collective-permute-start | bytes 3932168 | tf_op jit(solution)/shard_map/ppermute | solution.py:124
  247.3 59.1 %collective-permute-start.12 = (bf16[16,5120]{1,0:T(8,128)(2,1)S(1)}, bf16[16,5120]{1,0:T(8,128)(2,1)S(1)}, u32[]{:S(2)}, u32[]{:S(2)}) collective-permute-start(bf16[16,5120]{1,0:T(8,128)(2,1)S(1)} %slice.22), channel_id=1, source_target_pairs={{0,28},{4,24},{8,20},{12,16},{16,12},{20,8},{24,4},{28,0},{1,29},{... | collective-permute-start | bytes 491528 | tf_op jit(solution)/shard_map/ppermute | solution.py:109
  316.1 3.2 collective-permute-start.13
  317.6 21.0 %collective-permute-start.11 = (f32[160,2048]{1,0:T(8,128)S(1)}, f32[160,2048]{1,0:T(8,128)S(1)}, u32[]{:S(2)}, u32[]{:S(2)}) collective-permute-start(f32[160,2048]{1,0:T(8,128)S(1)} %add.100), channel_id=1, source_target_pairs={{1,3},{5,7},{8,10},{12,14},{19,17},{23,21},{26,24},{30,28}} | collective-permute-start | bytes 3932168 | tf_op jit(solution)/shard_map/ppermute | solution.py:124
  319.4 13.0 %copy-start.5 = (f32[320,2048]{1,0:T(8,128)S(1)}, f32[320,2048]{1,0:T(8,128)}, u32[]{:S(2)}) copy-start(f32[320,2048]{1,0:T(8,128)} %add.89) | copy-start | bytes 7864324
  330.5 2.0 copy-start.4
  330.5 5.0 %collective-permute-start.16 = (f32[144,2048]{1,0:T(8,128)S(1)}, f32[144,2048]{1,0:T(8,128)S(1)}, u32[]{:S(2)}, u32[]{:S(2)}) collective-permute-start(f32[144,2048]{1,0:T(8,128)S(1)} %shard_map.44), channel_id=1, source_target_pairs={{0,1},{2,3},{4,5},{6,7},{9,8},{11,10},{13,12},{15,14},{16,17},{18,... | collective-permute-start | bytes 3538952 | tf_op jit(solution)/shard_map/ppermute | solution.py:124
  335.7 18.4 %collective-permute-start.17 = (f32[144,2048]{1,0:T(8,128)S(1)}, f32[144,2048]{1,0:T(8,128)S(1)}, u32[]{:S(2)}, u32[]{:S(2)}) collective-permute-start(f32[144,2048]{1,0:T(8,128)S(1)} %add.108), channel_id=1, source_target_pairs={{1,3},{5,7},{8,10},{12,14},{19,17},{23,21},{26,24},{30,28}} | collective-permute-start | bytes 3538952 | tf_op jit(solution)/shard_map/ppermute | solution.py:124
  337.3 16.8 %collective-permute-start.14 = (f32[16,2048]{1,0:T(8,128)S(1)}, f32[16,2048]{1,0:T(8,128)S(1)}, u32[]{:S(2)}, u32[]{:S(2)}) collective-permute-start(f32[16,2048]{1,0:T(8,128)S(1)} %add.104), channel_id=1, source_target_pairs={{1,3},{5,7},{8,10},{12,14},{19,17},{23,21},{26,24},{30,28}} | collective-permute-start | bytes 393224 | tf_op jit(solution)/shard_map/ppermute | solution.py:124
  354.4 1.5 copy-start.3
